TPU v7x, 128 devices: a whole 4x4x4 slice. The times are simulated.
128 devices in a mesh: ctx: 32 (over z, y, core), tp: 4 (over x).
Axes of the slice: x: 4, y: 4, z: 4, core: 2. Of those that a mesh axis runs over, the one named last changes fastest.
Arguments:
- x_tokens: bfloat16 [16384, 4096], P('ctx', 'tp'), may hold values from -60 to 60
- w_query: bfloat16 [4096, 4096], P(None, 'tp'), may hold values from -0.09375 to 0.09375
- w_key: bfloat16 [4096, 1024], P(None, 'tp'), may hold values from -0.09375 to 0.09375
- w_value: bfloat16 [4096, 1024], P(None, 'tp'), may hold values from -0.09375 to 0.09375
- w_output: bfloat16 [4096, 4096], P('tp'), may hold values from -0.09375 to 0.09375
- pattern: int32 [128, 8], P('ctx'), may hold values from 0 to 127, as said below
- doc_lengths: int32 [16], replicated, may hold values from 1 to 10240, 16384 in all
Outputs:
- attn_out: bfloat16 [16384, 4096], P(('ctx', 'tp'))
Inputs may be any that keep to these rules, and one draw needn't show every extreme that they name: `pattern`: row q has 8 entries; the first is q itself and every entry is at most q; entries may repeat. The rows of one index of ctx (4 rows) name at most 2 distinct blocks held by any other index of ctx (index i holding blocks i * 4 onward), and exactly 2 of index 0 for every other index. Every row of an index i in the upper half of ctx names 2 blocks of index i minus half the number of ctx indices.
All inputs are finite; a program needn't handle non-finite values.
Results may differ from a plain program's by a relative error of at most 0.02.
Values may be sent and summed in bfloat16 or wider, within the bound.
No kernel may reach another device: no remote copies, remote signals or barrier semaphores. Data moves between devices by JAX's collectives and lax.ppermute only.
A program may use at most 128 MiB of HBM per device.

v0:
```python
import functools

import jax
import jax.numpy as jnp
from jax import lax
from jax.experimental import pallas as pl
from jax.experimental.pallas import tpu as pltpu
from jax.sharding import PartitionSpec as P

HD = 128
BLK = 128
LIST = 8
ROPE_BASE = 500000.0
NEG_LARGE = -1e30
CHUNKS = 2
VMEM = 20 << 20
BF16 = jnp.bfloat16
F32 = jnp.float32


def ctx_index(z, y, c):
    return ((z % 4) * 4 + (y % 4)) * 2 + c


def plane_pairs(step, first):
    pairs = []
    for z in range(4):
        for y in range(4):
            for c in range(2):
                along_z = (c == 0) == first
                to = ctx_index(z + step, y, c) if along_z else ctx_index(z, y + step, c)
                pairs.append((ctx_index(z, y, c), to))
    return pairs


CORE_PAIRS = [(i, i ^ 1) for i in range(32)]


def tp_pairs(step):
    return [(i, (i + step) % 4) for i in range(4)]


def core_swap(u):
    return lax.ppermute(u, "ctx", CORE_PAIRS)


def send_tp(u, step):
    return lax.ppermute(u, "tp", tp_pairs(step))


def send_one(u, step):
    return lax.ppermute(u, "ctx", plane_pairs(step, True))


def send_two(u, step):
    return lax.ppermute(u, "ctx", plane_pairs(step, False))


def roped(u, cosine, sine):
    return u * cosine + pltpu.roll(u, HD // 2, 1) * sine


def kv_kernel(ids, own, before, after, far, wk, wv, cos, sin, mine, theirs, tk, tv):
    step = pl.program_id(0)
    for at, ref in enumerate((own, before, after, far)):

        @pl.when(step == at)
        def _(at=at, ref=ref):
            for w, total in ((wk, tk), (wv, tv)):
                part = jnp.dot(ref[...], w[...], preferred_element_type=F32)
                if at == 0:
                    total[...] = part
                else:
                    total[...] += part

    @pl.when(step == 3)
    def _():
        cosine, sine = cos[...], sin[...]
        heads = [roped(tk[:, h * HD : (h + 1) * HD], cosine, sine).astype(BF16) for h in range(2)]
        vals = [tv[:, h * HD : (h + 1) * HD].astype(BF16) for h in range(2)]

        for core in range(2):

            @pl.when(ids[4] == core)
            def _(core=core):
                mine[:, :HD] = heads[core]
                mine[:, HD:] = vals[core]
                theirs[:, :HD] = heads[1 - core]
                theirs[:, HD:] = vals[1 - core]


def project_kv(ids, sources, wk, wv, cos, sin):
    rows, depth = sources[0].shape
    whole = lambda u: pl.BlockSpec(u.shape, lambda k, ids: (0, 0))
    w_spec = pl.BlockSpec((depth, 2 * HD), lambda k, ids: (ids[k], 0))
    out = jax.ShapeDtypeStruct((rows, 2 * HD), BF16)
    return pl.pallas_call(
        kv_kernel,
        grid_spec=pltpu.PrefetchScalarGridSpec(
            num_scalar_prefetch=1,
            grid=(4,),
            in_specs=[whole(u) for u in sources] + [w_spec, w_spec, whole(cos), whole(sin)],
            out_specs=[pl.BlockSpec((rows, 2 * HD), lambda k, ids: (0, 0))] * 2,
            scratch_shapes=[pltpu.VMEM((rows, 2 * HD), F32)] * 2,
        ),
        out_shape=[out, out],
        compiler_params=pltpu.CompilerParams(vmem_limit_bytes=VMEM),
        cost_estimate=pl.CostEstimate(
            flops=2 * rows * 4 * depth * 4 * HD, bytes_accessed=6 << 20, transcendentals=0
        ),
    )(ids, *sources, wk, wv, cos, sin)


def q_kernel(ids, *refs):
    parts, (wq, cos, sin, out) = [refs[4 * k : 4 * k + 4] for k in range(CHUNKS)], refs[4 * CHUNKS :]
    depth = parts[0][0].shape[1]
    at = [pl.ds(pl.multiple_of(ids[k] * depth, depth), depth) for k in range(4)]
    for chunk, sources in enumerate(parts):
        rows = sources[0].shape[0]
        span = slice(chunk * rows, (chunk + 1) * rows)
        total = sum(jnp.dot(sources[k][...], wq[at[k], :], preferred_element_type=F32) for k in range(4))
        cosine, sine = cos[span, :], sin[span, :]
        for h in range(2):
            turned = roped(total[:, h * HD : (h + 1) * HD], cosine, sine) * HD ** (-0.5)
            out[span, h * HD : (h + 1) * HD] = turned.astype(BF16)


def project_q(ids, side, sources, wq, cos, sin):
    rows, inner = cos.shape[0], wq.shape[0]
    flat = [u for part in sources for u in part]
    whole = lambda u: pl.BlockSpec(u.shape, lambda j, ids: (0, 0))
    return pl.pallas_call(
        q_kernel,
        grid_spec=pltpu.PrefetchScalarGridSpec(
            num_scalar_prefetch=1,
            grid=(2,),
            in_specs=[whole(u) for u in flat]
            + [
                pl.BlockSpec((inner, 2 * HD), lambda j, ids: (0, 2 * ids[4 + side] + j)),
                whole(cos),
                whole(sin),
            ],
            out_specs=pl.BlockSpec((rows, 2 * HD), lambda j, ids: (0, j)),
        ),
        out_shape=jax.ShapeDtypeStruct((rows, 4 * HD), BF16),
        compiler_params=pltpu.CompilerParams(vmem_limit_bytes=VMEM),
        cost_estimate=pl.CostEstimate(
            flops=2 * rows * inner * 4 * HD, bytes_accessed=8 << 20, transcendentals=0
        ),
    )(ids, *flat, wq, cos, sin)


def pack_kernel(*refs):
    parts, out = refs[:-1], refs[-1]
    rows = parts[0].shape[0]
    for k, u in enumerate(parts):
        out[k * rows : (k + 1) * rows, :] = u[...]


def pack(*parts):
    rows, cols = parts[0].shape
    vmem = pl.BlockSpec(memory_space=pltpu.VMEM)
    return pl.pallas_call(
        pack_kernel,
        in_specs=[vmem] * len(parts),
        out_specs=vmem,
        out_shape=jax.ShapeDtypeStruct((len(parts) * rows, cols), parts[0].dtype),
        compiler_params=pltpu.CompilerParams(vmem_limit_bytes=VMEM),
        cost_estimate=pl.CostEstimate(flops=0, bytes_accessed=2 * len(parts) * rows * cols * 2, transcendentals=0),
    )(*parts)


def attend_kernel(side, offsets, n_arrays, ids, table, lengths, query, *rest):
    arrays, (out, held) = rest[:n_arrays], rest[n_arrays:]
    count = len(offsets)
    blocks = [lax.rem(ids[0] + off, 4) for off in offsets]

    for n, block in enumerate(blocks):
        for e in range(LIST):
            place = table[(side * 4 + block) * LIST + e]
            to = slice((n * LIST + e) * BLK, (n * LIST + e + 1) * BLK)

            def from_array(ref, place=place, to=to):
                def go():
                    held[to, :] = ref[pl.ds(pl.multiple_of(lax.rem(place, 64) * BLK, BLK), BLK), :]

                return go

            lax.switch(lax.div(place, 64), [from_array(r) for r in arrays])

    rows = lax.broadcasted_iota(jnp.int32, (BLK, BLK), 0)
    lanes = lax.broadcasted_iota(jnp.int32, (BLK, BLK), 1)
    for n, block in enumerate(blocks):
        at = pl.ds(pl.multiple_of(block * BLK, BLK), BLK)
        position = rows + (ids[6 + side] + block * BLK)
        begin, end = jnp.zeros_like(rows), 0
        for d in range(lengths.shape[0]):
            end = end + lengths[d]
            begin = jnp.where(position >= end, end, begin)
        bias = []
        for e in range(LIST):
            index = lanes + table[(8 + side * 4 + block) * LIST + e]
            bias.append(jnp.where((index <= position) & (index >= begin), 0.0, NEG_LARGE))
        bias = jnp.concatenate(bias, axis=1)
        span = slice(n * LIST * BLK, (n + 1) * LIST * BLK)
        keys = held[span, :HD]
        values = held[span, HD:]
        part = jnp.concatenate([query[at, h * HD : (h + 1) * HD] for h in range(4)])
        scores = lax.dot_general(part, keys, (((1,), (1,)), ((), ())), preferred_element_type=F32)
        rounded, totals = [], []
        for h in range(4):
            masked = scores[h * BLK : (h + 1) * BLK] + bias
            weights = jnp.exp(masked - jnp.max(masked, axis=1, keepdims=True))
            totals.append(jnp.sum(weights, axis=1, keepdims=True))
            rounded.append(weights.astype(BF16))
        mixed = jnp.dot(jnp.concatenate(rounded), values, preferred_element_type=F32)
        for h in range(4):
            done = mixed[h * BLK : (h + 1) * BLK] / totals[h]
            out[n * BLK : (n + 1) * BLK, h * HD : (h + 1) * HD] = done.astype(BF16)


def attend(side, offsets, ids, table, lengths, query, arrays):
    count = len(offsets)
    smem = pl.BlockSpec(memory_space=pltpu.SMEM)
    vmem = pl.BlockSpec(memory_space=pltpu.VMEM)
    work = count * 4 * BLK * LIST * BLK
    return pl.pallas_call(
        functools.partial(attend_kernel, side, offsets, len(arrays)),
        in_specs=[smem] * 3 + [vmem] * (1 + len(arrays)),
        out_specs=vmem,
        out_shape=jax.ShapeDtypeStruct((count * BLK, 4 * HD), BF16),
        scratch_shapes=[pltpu.VMEM((count * LIST * BLK, 2 * HD), BF16)],
        compiler_params=pltpu.CompilerParams(vmem_limit_bytes=VMEM),
        cost_estimate=pl.CostEstimate(
            flops=4 * work * HD, bytes_accessed=count << 20, transcendentals=work
        ),
    )(ids, table, lengths, query, *arrays)


def heads_in_order(core, mine, other):
    return jnp.concatenate(
        [jnp.where(core == 0, mine, other), jnp.where(core == 0, other, mine)], axis=1
    )


def far_kernel(core, mine, other, w_left, w_right, left, right):
    rows = heads_in_order(core[0], mine[...], other[...])
    left[...] = jnp.dot(rows, w_left[...], preferred_element_type=F32).astype(BF16)
    right[...] = jnp.dot(rows, w_right[...], preferred_element_type=F32).astype(BF16)


TILE = 512


def project_far(core, mine, other, wo):
    rows, cols = mine.shape[0], wo.shape[1]
    n = cols // TILE // 2
    whole = pl.BlockSpec(mine.shape, lambda j, core: (0, 0))
    out = jax.ShapeDtypeStruct((rows, cols // 2), BF16)
    return pl.pallas_call(
        far_kernel,
        grid_spec=pltpu.PrefetchScalarGridSpec(
            num_scalar_prefetch=1,
            grid=(n,),
            in_specs=[
                whole,
                whole,
                pl.BlockSpec((wo.shape[0], TILE), lambda j, core: (0, j)),
                pl.BlockSpec((wo.shape[0], TILE), lambda j, core: (0, j + n)),
            ],
            out_specs=[pl.BlockSpec((rows, TILE), lambda j, core: (0, j))] * 2,
        ),
        out_shape=[out, out],
        compiler_params=pltpu.CompilerParams(vmem_limit_bytes=VMEM),
        cost_estimate=pl.CostEstimate(
            flops=2 * rows * wo.shape[0] * cols, bytes_accessed=10 << 20, transcendentals=0
        ),
    )(core, mine, other, wo, wo)


def near_kernel(n, core, mine, other, w, left, right, to_after, to_before):
    j = pl.program_id(0)
    rows = heads_in_order(core[0], mine[...], other[...])
    part = jnp.dot(rows, w[...], preferred_element_type=F32)

    @pl.when(j < n)
    def _():
        to_after[...] = (part[:BLK] + left[...].astype(F32)).astype(BF16)
        to_before[...] = part[BLK:].astype(BF16)

    @pl.when(j >= n)
    def _():
        to_after[...] = part[:BLK].astype(BF16)
        to_before[...] = (part[BLK:] + right[...].astype(F32)).astype(BF16)


def project_near(core, mine, other, wo, left, right):
    cols = wo.shape[1]
    n = cols // TILE // 2
    whole = pl.BlockSpec(mine.shape, lambda j, core: (0, 0))
    out = jax.ShapeDtypeStruct((BLK, cols), BF16)
    return pl.pallas_call(
        functools.partial(near_kernel, n),
        grid_spec=pltpu.PrefetchScalarGridSpec(
            num_scalar_prefetch=1,
            grid=(2 * n,),
            in_specs=[
                whole,
                whole,
                pl.BlockSpec((wo.shape[0], TILE), lambda j, core: (0, j)),
                pl.BlockSpec((BLK, TILE), lambda j, core: (0, jnp.minimum(j, n - 1))),
                pl.BlockSpec((BLK, TILE), lambda j, core: (0, jnp.maximum(j - n, 0))),
            ],
            out_specs=[pl.BlockSpec((BLK, TILE), lambda j, core: (0, j))] * 2,
        ),
        out_shape=[out, out],
        compiler_params=pltpu.CompilerParams(vmem_limit_bytes=VMEM),
        cost_estimate=pl.CostEstimate(
            flops=4 * BLK * wo.shape[0] * cols, bytes_accessed=11 << 20, transcendentals=0
        ),
    )(core, mine, other, wo, left, right)


def own_kernel(core, mine, other, w, out):
    rows = heads_in_order(core[0], mine[...], other[...])
    out[...] = jnp.dot(rows, w[...], preferred_element_type=F32)


def project_own(core, mine, other, wo):
    cols = wo.shape[1]
    whole = pl.BlockSpec(mine.shape, lambda j, core: (0, 0))
    return pl.pallas_call(
        own_kernel,
        grid_spec=pltpu.PrefetchScalarGridSpec(
            num_scalar_prefetch=1,
            grid=(cols // TILE,),
            in_specs=[whole, whole, pl.BlockSpec((wo.shape[0], TILE), lambda j, core: (0, j))],
            out_specs=pl.BlockSpec((BLK, TILE), lambda j, core: (0, j)),
        ),
        out_shape=jax.ShapeDtypeStruct((BLK, cols), F32),
        compiler_params=pltpu.CompilerParams(vmem_limit_bytes=VMEM),
        cost_estimate=pl.CostEstimate(
            flops=2 * BLK * wo.shape[0] * cols, bytes_accessed=10 << 20, transcendentals=0
        ),
    )(core, mine, other, wo)


def rope_tables(positions):
    frequency = ROPE_BASE ** (-(jnp.arange(HD // 2, dtype=F32) * 2.0 / HD))
    angles = positions.astype(F32)[:, None] * frequency[None, :]
    cosine, sine = jnp.cos(angles), jnp.sin(angles)
    return jnp.concatenate([cosine, cosine], axis=1), jnp.concatenate([-sine, sine], axis=1)


def fresh_entries(pattern):
    equal = pattern[:, :, None] == pattern[:, None, :]
    earlier = jnp.tril(jnp.ones((LIST, LIST), dtype=bool), -1)
    return jnp.logical_not(jnp.any(equal & earlier[None], axis=2))


def block_places(pattern, me):
    core, y, z = me % 2, (me // 2) % 4, me // 8
    per = 4 // CHUNKS
    chip = pattern // 8
    from_z, from_y = chip // 4, chip % 4
    other, local = ((pattern // 4) % 2 != core).astype(jnp.int32), pattern % 4
    along_one = jnp.where(core == 0, z - from_z, y - from_y) % 4
    along_two = jnp.where(core == 0, y - from_y, z - from_z) % 4
    slots = [jnp.where(u == 3, 2, jnp.where(u == 2, 3, u)) for u in (along_one, along_two)]
    array = (local // per) * 4 + slots[1]
    return array * 64 + (slots[0] * 2 + other) * per + local % per


def after(u, *others):
    return lax.optimization_barrier((u, *others))[0]


def on_device(x_tokens, w_query, w_key, w_value, w_output, pattern, doc_lengths):
    rows = x_tokens.shape[0]
    tp, me = lax.axis_index("tp"), lax.axis_index("ctx")
    core = me % 2
    length = rows // CHUNKS
    ids = jnp.stack(
        [tp, (tp + 3) % 4, (tp + 1) % 4, (tp + 2) % 4, core, 1 - core, me * rows, (me ^ 1) * rows]
    ).astype(jnp.int32)
    cos, sin = rope_tables(me * rows + jnp.arange(rows, dtype=jnp.int32))
    listed = jnp.concatenate([pattern, core_swap(pattern)])
    base = jnp.where(fresh_entries(listed), listed * BLK, 1 << 24)
    table = jnp.concatenate([block_places(listed, me), base]).astype(jnp.int32).reshape(-1)

    first, second = x_tokens[:length], x_tokens[length:]
    first_before, first_after = send_tp(first, 1), send_tp(first, -1)
    first_far = send_tp(after(first_before, ids, cos, sin, table), 1)
    second_after = send_tp(after(second, first_after), -1)
    second_before = send_tp(after(second, first_far), 1)
    second_far = send_tp(second_after, -1)
    sources = [
        (first, first_before, first_after, first_far),
        (second, second_before, second_after, second_far),
    ]

    gathered, query = [], []
    for chunk in range(CHUNKS):
        part = slice(chunk * length, (chunk + 1) * length)
        mine, theirs = project_kv(ids, sources[chunk], w_key, w_value, cos[part], sin[part])
        shard = pack(mine, core_swap(theirs))
        line = pack(shard, *[send_one(shard, step) for step in (1, -1, 2)])
        near = {step: send_two(line, step) for step in (1, -1)}
        made = project_q(ids, 1 - chunk, sources, w_query, cos, sin)
        query.append(made if chunk else core_swap(made))
        way = 1 - 2 * chunk
        gathered += [line, near[1], near[-1], send_two(after(near[way], made), way)]

    def attended(*offsets):
        other = core_swap(attend(1, offsets, ids, table, doc_lengths, query[0], gathered))
        return attend(0, offsets, ids, table, doc_lengths, query[1], gathered), other

    core_id = ids[4:5]
    left, right = project_far(core_id, *attended(2), w_output)
    left, right = send_tp(left, 1), send_tp(right, -1)
    to_after, to_before = project_near(core_id, *attended(1, 3), w_output, left, right)
    from_before, from_after = send_tp(to_after, 1), send_tp(to_before, -1)
    own = project_own(core_id, *attended(0), w_output)
    return (own + from_before.astype(F32) + from_after.astype(F32)).astype(BF16)


def solution(mesh):
    return jax.shard_map(
        on_device,
        mesh=mesh,
        in_specs=(
            P("ctx", "tp"),
            P(None, "tp"),
            P(None, "tp"),
            P(None, "tp"),
            P("tp", None),
            P("ctx", None),
            P(),
        ),
        out_specs=P(("ctx", "tp"), None),
        check_vma=False,
    )
```

profile of v0, /device:TPU:1, one launch (start us, length us, event | category | flops | bytes accessed | tf_op | source)
XLA Modules:
  0.0 167.4 jit_solution(16985379018972350629)
XLA Ops:
  0.0 1.3 fusion.31
  1.3 3.4 %collective-permute-start.2 = (bf16[256,1024]{1,0:T(8,128)(2,1)S(1)}, bf16[256,1024]{1,0:T(8,128)(2,1)}, u32[]{:S(2)}, u32[]{:S(2)}) collective-permute-start(bf16[256,1024]{1,0:T(8,128)(2,1)S(1)} %get-tuple-element.32.refs_0_.own), channel_id=1, source_target_pairs={{0,3},{1,0},{2,1},{3,2},{4,7},{5,4},{6,5},{7,6},{8,11},{9,8},{10,9... | collective-permute-start | bytes 1572872 | tf_op jit(solution)/shard_map/ppermute | solution.py:48
  4.7 1.0 collective-permute-start
  5.7 0.1 iota_compare_fusion
  5.7 1.0 fusion.4
  6.8 0.9 pad_maximum_fusion
  7.7 0.1 stack.35.ids
  7.8 0.3 and_reduce_fusion
  8.2 0.1 reshape.29.table
  8.3 10.2 %collective-permute-done.1.refs_1_.before = bf16[256,1024]{1,0:T(8,128)(2,1)} collective-permute-done((bf16[256,1024]{1,0:T(8,128)(2,1)S(1)}, bf16[256,1024]{1,0:T(8,128)(2,1)}, u32[]{:S(2)}, u32[]{:S(2)}) %collective-permute-start.1) | collective-permute-done | bytes 524320 | tf_op jit(solution)/shard_map/ppermute | solution.py:48
  18.5 2.7 %collective-permute-start.5 = (bf16[256,1024]{1,0:T(8,128)(2,1)S(1)}, bf16[256,1024]{1,0:T(8,128)(2,1)S(1)}, u32[]{:S(2)}, u32[]{:S(2)}) collective-permute-start(bf16[256,1024]{1,0:T(8,128)(2,1)S(1)} %get-tuple-element.20.refs_4_.own), channel_id=1, source_target_pairs={{0,3},{1,0},{2,1},{3,2},{4,7},{5,4},{6,5},{7,6},{8,11},{9,8},{10,9... | collective-permute-start | bytes 1572872 | tf_op jit(solution)/shard_map/ppermute | solution.py:48
  21.1 10.3 %collective-permute-done.3.refs_3_.far = bf16[256,1024]{1,0:T(8,128)(2,1)S(1)} collective-permute-done((bf16[256,1024]{1,0:T(8,128)(2,1)}, bf16[256,1024]{1,0:T(8,128)(2,1)S(1)}, u32[]{:S(2)}, u32[]{:S(2)}) %collective-permute-start.3) | collective-permute-done | bytes 524320 | tf_op jit(solution)/shard_map/ppermute | solution.py:48
  31.4 2.2 %collective-permute-start.6 = (bf16[256,1024]{1,0:T(8,128)(2,1)S(1)}, bf16[256,1024]{1,0:T(8,128)(2,1)S(1)}, u32[]{:S(2)}, u32[]{:S(2)}) collective-permute-start(bf16[256,1024]{1,0:T(8,128)(2,1)S(1)} %collective-permute-done.5.refs_6_.after), channel_id=1, source_target_pairs={{0,3},{1,0},{2,1},{3,2},{4,7},{5,4},{6,5},{7,6},{8,11},{9,8},{10,9... | collective-permute-start | bytes 1572872 | tf_op jit(solution)/shard_map/ppermute | solution.py:48
  33.6 1.5 fusion.1
  35.1 1.6 copy-done.1
  36.7 4.0 %shard_map.74 = (bf16[256,256]{1,0:T(8,128)(2,1)S(1)}, bf16[256,256]{1,0:T(8,128)(2,1)S(1)}) custom-call(s32[8]{0:T(128)S(1)} %stack.35.ids, bf16[256,1024]{1,0:T(8,128)(2,1)S(1)} %get-tuple-element.32.refs_0_.own, bf16[256,1024]{1,0:T(8,128)(2,1)} %collective-permute-done.1.refs_1_.before, bf16[256,1024]{1,0:T(8,128)(2,1)} %collective-permute-done.2.refs_2_.after, ...), custom_call_target="tpu_custom_call" | custom-call | flops 1073741824 | bytes 6291456 | tf_op jit(solution)/shard_map/pallas_call | solution.py:97
  40.7 3.4 %collective-permute-start.7 = (bf16[256,256]{1,0:T(8,128)(2,1)S(1)}, bf16[256,256]{1,0:T(8,128)(2,1)S(1)}, u32[]{:S(2)}, u32[]{:S(2)}) collective-permute-start(bf16[256,256]{1,0:T(8,128)(2,1)S(1)} %get-tuple-element.22), channel_id=1, source_target_pairs={{0,4},{4,0},{8,12},{12,8},{16,20},{20,16},{24,28},{28,24},{32,36},... | collective-permute-start | bytes 393224 | tf_op jit(solution)/shard_map/ppermute | solution.py:44
  44.2 1.0 collective-permute-done.7.refs_1_
  45.2 3.0 %collective-permute-start.10 = (bf16[512,256]{1,0:T(8,128)(2,1)S(1)}, bf16[512,256]{1,0:T(8,128)(2,1)S(1)}, u32[]{:S(2)}, u32[]{:S(2)}) collective-permute-start(bf16[512,256]{1,0:T(8,128)(2,1)S(1)} %shard_map.75.refs_0_), channel_id=1, source_target_pairs={{0,64},{4,20},{8,72},{12,28},{16,80},{20,4},{24,88},{28,12},{32,96... | collective-permute-start | bytes 786440 | tf_op jit(solution)/shard_map/ppermute | solution.py:52
  48.2 2.5 %shard_map.78 = (bf16[256,256]{1,0:T(8,128)(2,1)S(1)}, bf16[256,256]{1,0:T(8,128)(2,1)S(1)}) custom-call(s32[8]{0:T(128)S(1)} %stack.35.ids, bf16[256,1024]{1,0:T(8,128)(2,1)S(1)} %get-tuple-element.20.refs_4_.own, bf16[256,1024]{1,0:T(8,128)(2,1)S(1)} %collective-permute-done.4.refs_5_.before, bf16[256,1024]{1,0:T(8,128)(2,1)S(1)} %collective-permute-done.5.refs_6_.after, ...), custom_call_target="tpu_custom_call" | custom-call | flops 1073741824 | bytes 6291456 | tf_op jit(solution)/shard_map/pallas_call | solution.py:97
  50.7 1.4 collective-permute-start.14
  52.1 2.7 %collective-permute-start.9 = (bf16[512,256]{1,0:T(8,128)(2,1)S(1)}, bf16[512,256]{1,0:T(8,128)(2,1)S(1)}, u32[]{:S(2)}, u32[]{:S(2)}) collective-permute-start(bf16[512,256]{1,0:T(8,128)(2,1)S(1)} %shard_map.75.refs_0_), channel_id=1, source_target_pairs={{0,96},{4,28},{8,104},{12,4},{16,112},{20,12},{24,120},{28,20},{32... | collective-permute-start | bytes 786440 | tf_op jit(solution)/shard_map/ppermute | solution.py:52
  54.9 0.0 copy-start.2
  54.9 1.7 %collective-permute-start.17 = (bf16[512,256]{1,0:T(8,128)(2,1)S(1)}, bf16[512,256]{1,0:T(8,128)(2,1)S(1)}, u32[]{:S(2)}, u32[]{:S(2)}) collective-permute-start(bf16[512,256]{1,0:T(8,128)(2,1)S(1)} %shard_map.79.refs_0_), channel_id=1, source_target_pairs={{0,64},{4,20},{8,72},{12,28},{16,80},{20,4},{24,88},{28,12},{32,96... | collective-permute-start | bytes 786440 | tf_op jit(solution)/shard_map/ppermute | solution.py:52
  56.6 1.1 collective-permute-start.16
  57.7 0.5 collective-permute-start.15
  58.2 6.2 %collective-permute-done.8.refs_1_ = bf16[512,256]{1,0:T(8,128)(2,1)S(1)} collective-permute-done((bf16[512,256]{1,0:T(8,128)(2,1)S(1)}, bf16[512,256]{1,0:T(8,128)(2,1)S(1)}, u32[]{:S(2)}, u32[]{:S(2)}) %collective-permute-start.8) | collective-permute-done | bytes 262176 | tf_op jit(solution)/shard_map/ppermute | solution.py:52
  64.4 0.1 shard_map.76.rest_0_
  64.5 1.1 collective-permute-start.11
  65.5 1.6 collective-permute-done.15.refs_1_
  67.2 0.1 shard_map.80.rest_4_
  67.3 4.0 %collective-permute-start.19 = (bf16[2048,256]{1,0:T(8,128)(2,1)S(1)}, bf16[2048,256]{1,0:T(8,128)(2,1)S(1)}, u32[]{:S(2)}, u32[]{:S(2)}) collective-permute-start(bf16[2048,256]{1,0:T(8,128)(2,1)S(1)} %shard_map.80.rest_4_), channel_id=1, source_target_pairs={{0,24},{4,100},{8,0},{12,108},{16,8},{20,116},{24,16},{28,124},{32... | collective-permute-start | bytes 3145736 | tf_op jit(solution)/shard_map/ppermute | solution.py:56
  71.2 3.3 %collective-permute-start.12 = (bf16[2048,256]{1,0:T(8,128)(2,1)S(1)}, bf16[2048,256]{1,0:T(8,128)(2,1)S(1)}, u32[]{:S(2)}, u32[]{:S(2)}) collective-permute-start(bf16[2048,256]{1,0:T(8,128)(2,1)S(1)} %shard_map.76.rest_0_), channel_id=1, source_target_pairs={{0,24},{4,100},{8,0},{12,108},{16,8},{20,116},{24,16},{28,124},{32... | collective-permute-start | bytes 3145736 | tf_op jit(solution)/shard_map/ppermute | solution.py:56
  74.6 4.9 %shard_map.73.query = bf16[512,512]{1,0:T(8,128)(2,1)S(1)} custom-call(s32[8]{0:T(128)S(1)} %stack.35.ids, bf16[256,1024]{1,0:T(8,128)(2,1)S(1)} %get-tuple-element.32.refs_0_.own, bf16[256,1024]{1,0:T(8,128)(2,1)} %collective-permute-done.1.refs_1_.before, bf16[256,1024]{1,0:T(8,128)(2,1)} %collective-permute-done.2.refs_2_.after, ...), custom_call_target="tpu_custom_call" | custom-call | flops 2147483648 | bytes 8388608 | tf_op jit(solution)/shard_map/pallas_call | solution.py:132
  79.5 0.0 copy-start.3
  79.5 4.9 %shard_map.77 = bf16[512,512]{1,0:T(8,128)(2,1)S(1)} custom-call(s32[8]{0:T(128)S(1)} %stack.35.ids, bf16[256,1024]{1,0:T(8,128)(2,1)S(1)} %get-tuple-element.32.refs_0_.own, bf16[256,1024]{1,0:T(8,128)(2,1)} %collective-permute-done.1.refs_1_.before, bf16[256,1024]{1,0:T(8,128)(2,1)} %collective-permute-done.2.refs_2_.after, ...), custom_call_target="tpu_custom_call" | custom-call | flops 2147483648 | bytes 8388608 | tf_op jit(solution)/shard_map/pallas_call | solution.py:132
  84.4 0.1 collective-permute-start.18
  84.5 0.1 collective-permute-start.13
  84.6 2.7 %collective-permute-start.20 = (bf16[2048,256]{1,0:T(8,128)(2,1)S(1)}, bf16[2048,256]{1,0:T(8,128)(2,1)S(1)}, u32[]{:S(2)}, u32[]{:S(2)}) collective-permute-start(bf16[2048,256]{1,0:T(8,128)(2,1)S(1)} %collective-permute-done.19.rest_6_), channel_id=1, source_target_pairs={{0,24},{4,100},{8,0},{12,108},{16,8},{20,116},{24,16},{28,124},{32... | collective-permute-start | bytes 3145736 | tf_op jit(solution)/shard_map/ppermute | solution.py:56
  87.3 3.9 %collective-permute-start.21 = (bf16[512,512]{1,0:T(8,128)(2,1)S(1)}, bf16[512,512]{1,0:T(8,128)(2,1)S(1)}, u32[]{:S(2)}, u32[]{:S(2)}) collective-permute-start(bf16[512,512]{1,0:T(8,128)(2,1)S(1)} %shard_map.77), channel_id=1, source_target_pairs={{0,4},{4,0},{8,12},{12,8},{16,20},{20,16},{24,28},{28,24},{32,36},... | collective-permute-start | bytes 1572872 | tf_op jit(solution)/shard_map/ppermute | solution.py:44
  91.2 1.5 collective-permute-done.21.query
  92.7 1.6 collective-permute-done.12.rest_2_
  94.3 5.4 %collective-permute-done.18.rest_5_ = bf16[2048,256]{1,0:T(8,128)(2,1)S(1)} collective-permute-done((bf16[2048,256]{1,0:T(8,128)(2,1)S(1)}, bf16[2048,256]{1,0:T(8,128)(2,1)S(1)}, u32[]{:S(2)}, u32[]{:S(2)}) %collective-permute-start.18) | collective-permute-done | bytes 1048608 | tf_op jit(solution)/shard_map/ppermute | solution.py:56
  99.7 11.2 %collective-permute-done.13.rest_3_ = bf16[2048,256]{1,0:T(8,128)(2,1)S(1)} collective-permute-done((bf16[2048,256]{1,0:T(8,128)(2,1)S(1)}, bf16[2048,256]{1,0:T(8,128)(2,1)S(1)}, u32[]{:S(2)}, u32[]{:S(2)}) %collective-permute-start.13) | collective-permute-done | bytes 1048608 | tf_op jit(solution)/shard_map/ppermute | solution.py:56
  110.9 2.4 %shard_map.87 = bf16[128,512]{1,0:T(8,128)(2,1)S(1)} custom-call(s32[8]{0:T(128)S(1)} %stack.35.ids, s32[128]{0:T(128)S(1)} %reshape.29.table, s32[16]{0:T(128)S(1)} %copy-done.3, bf16[512,512]{1,0:T(8,128)(2,1)S(1)} %collective-permute-done.21.query, bf16[2048,256]{1,0:T(8,128)(2,1)S(1)} %shard_map.76.rest_0_, ...), custom_call_target="tpu_custom_call" | custom-call | flops 268435456 | bytes 1048576 | tf_op jit(solution)/shard_map/pallas_call | solution.py:227
  113.3 0.0 slice-start.1
  113.3 3.3 %collective-permute-start.24 = (bf16[128,512]{1,0:T(8,128)(2,1)S(1)}, bf16[128,512]{1,0:T(8,128)(2,1)S(1)}, u32[]{:S(2)}, u32[]{:S(2)}) collective-permute-start(bf16[128,512]{1,0:T(8,128)(2,1)S(1)} %shard_map.87), channel_id=1, source_target_pairs={{0,4},{4,0},{8,12},{12,8},{16,20},{20,16},{24,28},{28,24},{32,36},... | collective-permute-start | bytes 393224 | tf_op jit(solution)/shard_map/ppermute | solution.py:44
  116.6 2.3 %shard_map.86.mine = bf16[128,512]{1,0:T(8,128)(2,1)S(1)} custom-call(s32[8]{0:T(128)S(1)} %stack.35.ids, s32[128]{0:T(128)S(1)} %reshape.29.table, s32[16]{0:T(128)S(1)} %copy-done.3, bf16[512,512]{1,0:T(8,128)(2,1)S(1)} %shard_map.73.query, bf16[2048,256]{1,0:T(8,128)(2,1)S(1)} %shard_map.76.rest_0_, ...), custom_call_target="tpu_custom_call" | custom-call | flops 268435456 | bytes 1048576 | tf_op jit(solution)/shard_map/pallas_call | solution.py:227
  118.9 2.6 %shard_map.88 = (bf16[128,2048]{1,0:T(8,128)(2,1)S(1)}, bf16[128,2048]{1,0:T(8,128)(2,1)S(1)}) custom-call(s32[1]{0:T(128)} %bitcast.core, bf16[128,512]{1,0:T(8,128)(2,1)S(1)} %shard_map.86.mine, bf16[128,512]{1,0:T(8,128)(2,1)S(1)} %collective-permute-done.24.other, bf16[1024,4096]{1,0:T(8,128)(2,1)S(1)} %bitcast.9, bf16[1024,4096]{1,0:T(8,128)(2,1)S(1)} %bitcast.9), custom_call_target="tpu_custom_call" | custom-call | flops 1073741824 | bytes 10485760 | tf_op jit(solution)/shard_map/pallas_call | solution.py:260
  121.5 0.1 collective-permute-start.25
  121.6 2.7 %collective-permute-start.26 = (bf16[128,2048]{1,0:T(8,128)(2,1)S(1)}, bf16[128,2048]{1,0:T(8,128)(2,1)S(1)}, u32[]{:S(2)}, u32[]{:S(2)}) collective-permute-start(bf16[128,2048]{1,0:T(8,128)(2,1)S(1)} %get-tuple-element.28), channel_id=1, source_target_pairs={{0,3},{1,0},{2,1},{3,2},{4,7},{5,4},{6,5},{7,6},{8,11},{9,8},{10,9... | collective-permute-start | bytes 1572872 | tf_op jit(solution)/shard_map/ppermute | solution.py:48
  124.3 3.5 %shard_map.85 = bf16[256,512]{1,0:T(8,128)(2,1)S(1)} custom-call(s32[8]{0:T(128)S(1)} %stack.35.ids, s32[128]{0:T(128)S(1)} %reshape.29.table, s32[16]{0:T(128)S(1)} %copy-done.3, bf16[512,512]{1,0:T(8,128)(2,1)S(1)} %collective-permute-done.21.query, bf16[2048,256]{1,0:T(8,128)(2,1)S(1)} %shard_map.76.rest_0_, ...), custom_call_target="tpu_custom_call" | custom-call | flops 536870912 | bytes 2097152 | tf_op jit(solution)/shard_map/pallas_call | solution.py:227
  127.7 0.7 collective-permute-start.23
  128.4 3.1 %shard_map.84.mine = bf16[256,512]{1,0:T(8,128)(2,1)S(1)} custom-call(s32[8]{0:T(128)S(1)} %stack.35.ids, s32[128]{0:T(128)S(1)} %reshape.29.table, s32[16]{0:T(128)S(1)} %copy-done.3, bf16[512,512]{1,0:T(8,128)(2,1)S(1)} %shard_map.73.query, bf16[2048,256]{1,0:T(8,128)(2,1)S(1)} %shard_map.76.rest_0_, ...), custom_call_target="tpu_custom_call" | custom-call | flops 536870912 | bytes 2097152 | tf_op jit(solution)/shard_map/pallas_call | solution.py:227
  131.5 4.7 %collective-permute-done.25.left = bf16[128,2048]{1,0:T(8,128)(2,1)S(1)} collective-permute-done((bf16[128,2048]{1,0:T(8,128)(2,1)S(1)}, bf16[128,2048]{1,0:T(8,128)(2,1)S(1)}, u32[]{:S(2)}, u32[]{:S(2)}) %collective-permute-start.25) | collective-permute-done | bytes 524320 | tf_op jit(solution)/shard_map/ppermute | solution.py:48
  136.2 4.9 %shard_map.89 = (bf16[128,4096]{1,0:T(8,128)(2,1)S(1)}, bf16[128,4096]{1,0:T(8,128)(2,1)S(1)}) custom-call(s32[1]{0:T(128)} %bitcast.core, bf16[256,512]{1,0:T(8,128)(2,1)S(1)} %shard_map.84.mine, bf16[256,512]{1,0:T(8,128)(2,1)S(1)} %collective-permute-done.23.other, bf16[1024,4096]{1,0:T(8,128)(2,1)S(1)} %bitcast.9, ...), custom_call_target="tpu_custom_call" | custom-call | flops 2147483648 | bytes 11534336 | tf_op jit(solution)/shard_map/pallas_call | solution.py:302
  141.0 0.1 collective-permute-start.27
  141.1 2.7 %collective-permute-start.28 = (bf16[128,4096]{1,0:T(8,128)(2,1)S(1)}, bf16[128,4096]{1,0:T(8,128)(2,1)S(1)}, u32[]{:S(2)}, u32[]{:S(2)}) collective-permute-start(bf16[128,4096]{1,0:T(8,128)(2,1)S(1)} %get-tuple-element.30), channel_id=1, source_target_pairs={{0,3},{1,0},{2,1},{3,2},{4,7},{5,4},{6,5},{7,6},{8,11},{9,8},{10,9... | collective-permute-start | bytes 3145736 | tf_op jit(solution)/shard_map/ppermute | solution.py:48
  143.8 2.2 %shard_map.82 = bf16[128,512]{1,0:T(8,128)(2,1)S(1)} custom-call(s32[8]{0:T(128)S(1)} %stack.35.ids, s32[128]{0:T(128)S(1)} %reshape.29.table, s32[16]{0:T(128)S(1)} %copy-done.3, bf16[512,512]{1,0:T(8,128)(2,1)S(1)} %collective-permute-done.21.query, bf16[2048,256]{1,0:T(8,128)(2,1)S(1)} %shard_map.76.rest_0_, ...), custom_call_target="tpu_custom_call" | custom-call | flops 268435456 | bytes 1048576 | tf_op jit(solution)/shard_map/pallas_call | solution.py:227
  146.0 1.6 collective-permute-start.22
  147.6 2.2 %shard_map.81.mine = bf16[128,512]{1,0:T(8,128)(2,1)S(1)} custom-call(s32[8]{0:T(128)S(1)} %stack.35.ids, s32[128]{0:T(128)S(1)} %reshape.29.table, s32[16]{0:T(128)S(1)} %copy-done.3, bf16[512,512]{1,0:T(8,128)(2,1)S(1)} %shard_map.73.query, bf16[2048,256]{1,0:T(8,128)(2,1)S(1)} %shard_map.76.rest_0_, ...), custom_call_target="tpu_custom_call" | custom-call | flops 268435456 | bytes 1048576 | tf_op jit(solution)/shard_map/pallas_call | solution.py:227
  149.9 3.3 %shard_map.83 = f32[128,4096]{1,0:T(8,128)S(1)} custom-call(s32[1]{0:T(128)} %bitcast.core, bf16[128,512]{1,0:T(8,128)(2,1)S(1)} %shard_map.81.mine, bf16[128,512]{1,0:T(8,128)(2,1)S(1)} %collective-permute-done.22.other, bf16[1024,4096]{1,0:T(8,128)(2,1)S(1)} %bitcast.9), custom_call_target="tpu_custom_call" | custom-call | flops 1073741824 | bytes 10485760 | tf_op jit(solution)/shard_map/pallas_call | solution.py:332
  153.2 12.8 %collective-permute-done.27 = bf16[128,4096]{1,0:T(8,128)(2,1)S(1)} collective-permute-done((bf16[128,4096]{1,0:T(8,128)(2,1)S(1)}, bf16[128,4096]{1,0:T(8,128)(2,1)S(1)}, u32[]{:S(2)}, u32[]{:S(2)}) %collective-permute-start.27) | collective-permute-done | bytes 1048608 | tf_op jit(solution)/shard_map/ppermute | solution.py:48
  166.0 1.3 add_convert_fusion
  (52 shorter events, 0.2 us)
Async XLA Ops:
  0.0 4.7 %copy-start.7 = (s32[4,8]{1,0:T(4,128)S(1)}, s32[4,8]{1,0:T(4,128)}, u32[]{:S(2)}) copy-start(s32[4,8]{1,0:T(4,128)} %param.12) | copy-start | bytes 388
  1.3 33.8 %copy-start = (bf16[4096,256]{1,0:T(8,128)(2,1)S(1)}, bf16[4096,256]{1,0:T(8,128)(2,1)}, u32[]{:S(2)}) copy-start(bf16[4096,256]{1,0:T(8,128)(2,1)} %wk.3) | copy-start | bytes 6291460
  1.3 17.2 %collective-permute-start.2 = (bf16[256,1024]{1,0:T(8,128)(2,1)S(1)}, bf16[256,1024]{1,0:T(8,128)(2,1)}, u32[]{:S(2)}, u32[]{:S(2)}) collective-permute-start(bf16[256,1024]{1,0:T(8,128)(2,1)S(1)} %get-tuple-element.32.refs_0_.own), channel_id=1, source_target_pairs={{0,3},{1,0},{2,1},{3,2},{4,7},{5,4},{6,5},{7,6},{8,11},{9,8},{10,9... | collective-permute-start | bytes 1572872 | tf_op jit(solution)/shard_map/ppermute | solution.py:48
  4.7 13.8 %collective-permute-start.1 = (bf16[256,1024]{1,0:T(8,128)(2,1)S(1)}, bf16[256,1024]{1,0:T(8,128)(2,1)}, u32[]{:S(2)}, u32[]{:S(2)}) collective-permute-start(bf16[256,1024]{1,0:T(8,128)(2,1)S(1)} %get-tuple-element.32.refs_0_.own), channel_id=1, source_target_pairs={{0,1},{1,2},{2,3},{3,0},{4,5},{5,6},{6,7},{7,4},{8,9},{9,10},{10,1... | collective-permute-start | bytes 1572872 | tf_op jit(solution)/shard_map/ppermute | solution.py:48
  4.7 3.1 %collective-permute-start = (s32[4,8]{1,0:T(4,128)S(1)}, s32[4,8]{1,0:T(4,128)S(1)}, u32[]{:S(2)}, u32[]{:S(2)}) collective-permute-start(s32[4,8]{1,0:T(4,128)S(1)} %copy-done.7), channel_id=1, source_target_pairs={{0,4},{4,0},{8,12},{12,8},{16,20},{20,16},{24,28},{28,24},{32,36},... | collective-permute-start | bytes 392 | tf_op jit(solution)/shard_map/ppermute | solution.py:44
  6.7 1.0 copy-start.4
  6.8 1.0 copy-start.5
  6.8 0.9 copy-start.6
  18.5 13.0 %collective-permute-start.3 = (bf16[256,1024]{1,0:T(8,128)(2,1)}, bf16[256,1024]{1,0:T(8,128)(2,1)S(1)}, u32[]{:S(2)}, u32[]{:S(2)}) collective-permute-start(bf16[256,1024]{1,0:T(8,128)(2,1)} %collective-permute-done.1.refs_1_.before), channel_id=1, source_target_pairs={{0,1},{1,2},{2,3},{3,0},{4,5},{5,6},{6,7},{7,4},{8,9},{9,10},{10,1... | collective-permute-start | bytes 1572872 | tf_op jit(solution)/shard_map/ppermute | solution.py:48
  18.5 13.0 %collective-permute-start.5 = (bf16[256,1024]{1,0:T(8,128)(2,1)S(1)}, bf16[256,1024]{1,0:T(8,128)(2,1)S(1)}, u32[]{:S(2)}, u32[]{:S(2)}) collective-permute-start(bf16[256,1024]{1,0:T(8,128)(2,1)S(1)} %get-tuple-element.20.refs_4_.own), channel_id=1, source_target_pairs={{0,3},{1,0},{2,1},{3,2},{4,7},{5,4},{6,5},{7,6},{8,11},{9,8},{10,9... | collective-permute-start | bytes 1572872 | tf_op jit(solution)/shard_map/ppermute | solution.py:48
  31.4 16.7 %collective-permute-start.6 = (bf16[256,1024]{1,0:T(8,128)(2,1)S(1)}, bf16[256,1024]{1,0:T(8,128)(2,1)S(1)}, u32[]{:S(2)}, u32[]{:S(2)}) collective-permute-start(bf16[256,1024]{1,0:T(8,128)(2,1)S(1)} %collective-permute-done.5.refs_6_.after), channel_id=1, source_target_pairs={{0,3},{1,0},{2,1},{3,2},{4,7},{5,4},{6,5},{7,6},{8,11},{9,8},{10,9... | collective-permute-start | bytes 1572872 | tf_op jit(solution)/shard_map/ppermute | solution.py:48
  33.6 14.5 %collective-permute-start.4 = (bf16[256,1024]{1,0:T(8,128)(2,1)S(1)}, bf16[256,1024]{1,0:T(8,128)(2,1)S(1)}, u32[]{:S(2)}, u32[]{:S(2)}) collective-permute-start(bf16[256,1024]{1,0:T(8,128)(2,1)S(1)} %get-tuple-element.20.refs_4_.own), channel_id=1, source_target_pairs={{0,1},{1,2},{2,3},{3,0},{4,5},{5,6},{6,7},{7,4},{8,9},{9,10},{10,1... | collective-permute-start | bytes 1572872 | tf_op jit(solution)/shard_map/ppermute | solution.py:48
  35.1 1.6 copy-start.1
  36.7 37.8 %slice-start.2 = ((s8[8388608]{0:T(1024)(128)(4,1)}), s8[4194304]{0:T(1024)(128)(4,1)S(1)}, s32[]{:S(2)}) async-start(s8[8388608]{0:T(1024)(128)(4,1)} %bitcast.10), calls=%async_computation.2 | async-start | bytes 8388608
  40.7 4.4 %collective-permute-start.7 = (bf16[256,256]{1,0:T(8,128)(2,1)S(1)}, bf16[256,256]{1,0:T(8,128)(2,1)S(1)}, u32[]{:S(2)}, u32[]{:S(2)}) collective-permute-start(bf16[256,256]{1,0:T(8,128)(2,1)S(1)} %get-tuple-element.22), channel_id=1, source_target_pairs={{0,4},{4,0},{8,12},{12,8},{16,20},{20,16},{24,28},{28,24},{32,36},... | collective-permute-start | bytes 393224 | tf_op jit(solution)/shard_map/ppermute | solution.py:44
  45.2 12.5 %collective-permute-start.10 = (bf16[512,256]{1,0:T(8,128)(2,1)S(1)}, bf16[512,256]{1,0:T(8,128)(2,1)S(1)}, u32[]{:S(2)}, u32[]{:S(2)}) collective-permute-start(bf16[512,256]{1,0:T(8,128)(2,1)S(1)} %shard_map.75.refs_0_), channel_id=1, source_target_pairs={{0,64},{4,20},{8,72},{12,28},{16,80},{20,4},{24,88},{28,12},{32,96... | collective-permute-start | bytes 786440 | tf_op jit(solution)/shard_map/ppermute | solution.py:52
  48.2 26.4 %slice-start.3 = ((s8[8388608]{0:T(1024)(128)(4,1)}), s8[4194304]{0:T(1024)(128)(4,1)S(1)}, s32[]{:S(2)}) async-start(s8[8388608]{0:T(1024)(128)(4,1)} %bitcast.10), calls=%async_computation.3 | async-start | bytes 8388608
  50.7 4.1 %collective-permute-start.14 = (bf16[256,256]{1,0:T(8,128)(2,1)S(1)}, bf16[256,256]{1,0:T(8,128)(2,1)S(1)}, u32[]{:S(2)}, u32[]{:S(2)}) collective-permute-start(bf16[256,256]{1,0:T(8,128)(2,1)S(1)} %get-tuple-element.25), channel_id=1, source_target_pairs={{0,4},{4,0},{8,12},{12,8},{16,20},{20,16},{24,28},{28,24},{32,36},... | collective-permute-start | bytes 393224 | tf_op jit(solution)/shard_map/ppermute | solution.py:44
  52.1 6.1 %collective-permute-start.9 = (bf16[512,256]{1,0:T(8,128)(2,1)S(1)}, bf16[512,256]{1,0:T(8,128)(2,1)S(1)}, u32[]{:S(2)}, u32[]{:S(2)}) collective-permute-start(bf16[512,256]{1,0:T(8,128)(2,1)S(1)} %shard_map.75.refs_0_), channel_id=1, source_target_pairs={{0,96},{4,28},{8,104},{12,4},{16,112},{20,12},{24,120},{28,20},{32... | collective-permute-start | bytes 786440 | tf_op jit(solution)/shard_map/ppermute | solution.py:52
  54.8 9.5 %collective-permute-start.8 = (bf16[512,256]{1,0:T(8,128)(2,1)S(1)}, bf16[512,256]{1,0:T(8,128)(2,1)S(1)}, u32[]{:S(2)}, u32[]{:S(2)}) collective-permute-start(bf16[512,256]{1,0:T(8,128)(2,1)S(1)} %shard_map.75.refs_0_), channel_id=1, source_target_pairs={{0,32},{4,12},{8,40},{12,20},{16,48},{20,28},{24,56},{28,4},{32,64... | collective-permute-start | bytes 786440 | tf_op jit(solution)/shard_map/ppermute | solution.py:52
  54.9 19.7 %copy-start.2 = (f32[512,128]{1,0:T(8,128)S(1)}, f32[512,128]{1,0:T(8,128)}, u32[]{:S(2)}) copy-start(f32[512,128]{1,0:T(8,128)} %get-tuple-element.43.refs_10_) | copy-start | bytes 786436
  54.9 10.7 %collective-permute-start.17 = (bf16[512,256]{1,0:T(8,128)(2,1)S(1)}, bf16[512,256]{1,0:T(8,128)(2,1)S(1)}, u32[]{:S(2)}, u32[]{:S(2)}) collective-permute-start(bf16[512,256]{1,0:T(8,128)(2,1)S(1)} %shard_map.79.refs_0_), channel_id=1, source_target_pairs={{0,64},{4,20},{8,72},{12,28},{16,80},{20,4},{24,88},{28,12},{32,96... | collective-permute-start | bytes 786440 | tf_op jit(solution)/shard_map/ppermute | solution.py:52
  56.6 8.9 %collective-permute-start.16 = (bf16[512,256]{1,0:T(8,128)(2,1)S(1)}, bf16[512,256]{1,0:T(8,128)(2,1)S(1)}, u32[]{:S(2)}, u32[]{:S(2)}) collective-permute-start(bf16[512,256]{1,0:T(8,128)(2,1)S(1)} %shard_map.79.refs_0_), channel_id=1, source_target_pairs={{0,96},{4,28},{8,104},{12,4},{16,112},{20,12},{24,120},{28,20},{32... | collective-permute-start | bytes 786440 | tf_op jit(solution)/shard_map/ppermute | solution.py:52
  57.7 9.5 %collective-permute-start.15 = (bf16[512,256]{1,0:T(8,128)(2,1)S(1)}, bf16[512,256]{1,0:T(8,128)(2,1)S(1)}, u32[]{:S(2)}, u32[]{:S(2)}) collective-permute-start(bf16[512,256]{1,0:T(8,128)(2,1)S(1)} %shard_map.79.refs_0_), channel_id=1, source_target_pairs={{0,32},{4,12},{8,40},{12,20},{16,48},{20,28},{24,56},{28,4},{32,64... | collective-permute-start | bytes 786440 | tf_op jit(solution)/shard_map/ppermute | solution.py:52
  64.5 20.1 %collective-permute-start.11 = (bf16[2048,256]{1,0:T(8,128)(2,1)S(1)}, bf16[2048,256]{1,0:T(8,128)(2,1)S(1)}, u32[]{:S(2)}, u32[]{:S(2)}) collective-permute-start(bf16[2048,256]{1,0:T(8,128)(2,1)S(1)} %shard_map.76.rest_0_), channel_id=1, source_target_pairs={{0,8},{4,36},{8,16},{12,44},{16,24},{20,52},{24,0},{28,60},{32,40}... | collective-permute-start | bytes 3145736 | tf_op jit(solution)/shard_map/ppermute | solution.py:56
  67.3 17.4 %collective-permute-start.19 = (bf16[2048,256]{1,0:T(8,128)(2,1)S(1)}, bf16[2048,256]{1,0:T(8,128)(2,1)S(1)}, u32[]{:S(2)}, u32[]{:S(2)}) collective-permute-start(bf16[2048,256]{1,0:T(8,128)(2,1)S(1)} %shard_map.80.rest_4_), channel_id=1, source_target_pairs={{0,24},{4,100},{8,0},{12,108},{16,8},{20,116},{24,16},{28,124},{32... | collective-permute-start | bytes 3145736 | tf_op jit(solution)/shard_map/ppermute | solution.py:56
  71.2 23.0 %collective-permute-start.12 = (bf16[2048,256]{1,0:T(8,128)(2,1)S(1)}, bf16[2048,256]{1,0:T(8,128)(2,1)S(1)}, u32[]{:S(2)}, u32[]{:S(2)}) collective-permute-start(bf16[2048,256]{1,0:T(8,128)(2,1)S(1)} %shard_map.76.rest_0_), channel_id=1, source_target_pairs={{0,24},{4,100},{8,0},{12,108},{16,8},{20,116},{24,16},{28,124},{32... | collective-permute-start | bytes 3145736 | tf_op jit(solution)/shard_map/ppermute | solution.py:56
  79.5 31.4 %copy-start.3 = (s32[16]{0:T(128)S(1)}, s32[16]{0:T(128)}, u32[]{:S(2)}) copy-start(s32[16]{0:T(128)} %lengths.11) | copy-start | bytes 196
  84.4 15.2 %collective-permute-start.18 = (bf16[2048,256]{1,0:T(8,128)(2,1)S(1)}, bf16[2048,256]{1,0:T(8,128)(2,1)S(1)}, u32[]{:S(2)}, u32[]{:S(2)}) collective-permute-start(bf16[2048,256]{1,0:T(8,128)(2,1)S(1)} %shard_map.80.rest_4_), channel_id=1, source_target_pairs={{0,8},{4,36},{8,16},{12,44},{16,24},{20,52},{24,0},{28,60},{32,40}... | collective-permute-start | bytes 3145736 | tf_op jit(solution)/shard_map/ppermute | solution.py:56
  84.5 26.4 %collective-permute-start.13 = (bf16[2048,256]{1,0:T(8,128)(2,1)S(1)}, bf16[2048,256]{1,0:T(8,128)(2,1)S(1)}, u32[]{:S(2)}, u32[]{:S(2)}) collective-permute-start(bf16[2048,256]{1,0:T(8,128)(2,1)S(1)} %collective-permute-done.11.rest_1_), channel_id=1, source_target_pairs={{0,8},{4,36},{8,16},{12,44},{16,24},{20,52},{24,0},{28,60},{32,40}... | collective-permute-start | bytes 3145736 | tf_op jit(solution)/shard_map/ppermute | solution.py:56
  84.6 26.3 %collective-permute-start.20 = (bf16[2048,256]{1,0:T(8,128)(2,1)S(1)}, bf16[2048,256]{1,0:T(8,128)(2,1)S(1)}, u32[]{:S(2)}, u32[]{:S(2)}) collective-permute-start(bf16[2048,256]{1,0:T(8,128)(2,1)S(1)} %collective-permute-done.19.rest_6_), channel_id=1, source_target_pairs={{0,24},{4,100},{8,0},{12,108},{16,8},{20,116},{24,16},{28,124},{32... | collective-permute-start | bytes 3145736 | tf_op jit(solution)/shard_map/ppermute | solution.py:56
  87.3 5.4 %collective-permute-start.21 = (bf16[512,512]{1,0:T(8,128)(2,1)S(1)}, bf16[512,512]{1,0:T(8,128)(2,1)S(1)}, u32[]{:S(2)}, u32[]{:S(2)}) collective-permute-start(bf16[512,512]{1,0:T(8,128)(2,1)S(1)} %shard_map.77), channel_id=1, source_target_pairs={{0,4},{4,0},{8,12},{12,8},{16,20},{20,16},{24,28},{28,24},{32,36},... | collective-permute-start | bytes 1572872 | tf_op jit(solution)/shard_map/ppermute | solution.py:44
  110.9 8.0 %slice-start = ((s8[8388608]{0:T(1024)(128)(4,1)}), s8[4194304]{0:T(1024)(128)(4,1)S(1)}, s32[]{:S(2)}) async-start(s8[8388608]{0:T(1024)(128)(4,1)} %bitcast.8), calls=%async_computation | async-start | bytes 8388608
  113.3 5.5 %slice-start.1 = ((s8[8388608]{0:T(1024)(128)(4,1)}), s8[4194304]{0:T(1024)(128)(4,1)S(1)}, s32[]{:S(2)}) async-start(s8[8388608]{0:T(1024)(128)(4,1)} %bitcast.8), calls=%async_computation.1 | async-start | bytes 8388608
  113.3 5.5 %collective-permute-start.24 = (bf16[128,512]{1,0:T(8,128)(2,1)S(1)}, bf16[128,512]{1,0:T(8,128)(2,1)S(1)}, u32[]{:S(2)}, u32[]{:S(2)}) collective-permute-start(bf16[128,512]{1,0:T(8,128)(2,1)S(1)} %shard_map.87), channel_id=1, source_target_pairs={{0,4},{4,0},{8,12},{12,8},{16,20},{20,16},{24,28},{28,24},{32,36},... | collective-permute-start | bytes 393224 | tf_op jit(solution)/shard_map/ppermute | solution.py:44
  121.5 14.7 %collective-permute-start.25 = (bf16[128,2048]{1,0:T(8,128)(2,1)S(1)}, bf16[128,2048]{1,0:T(8,128)(2,1)S(1)}, u32[]{:S(2)}, u32[]{:S(2)}) collective-permute-start(bf16[128,2048]{1,0:T(8,128)(2,1)S(1)} %get-tuple-element.27), channel_id=1, source_target_pairs={{0,1},{1,2},{2,3},{3,0},{4,5},{5,6},{6,7},{7,4},{8,9},{9,10},{10,1... | collective-permute-start | bytes 1572872 | tf_op jit(solution)/shard_map/ppermute | solution.py:48
  121.6 14.6 %collective-permute-start.26 = (bf16[128,2048]{1,0:T(8,128)(2,1)S(1)}, bf16[128,2048]{1,0:T(8,128)(2,1)S(1)}, u32[]{:S(2)}, u32[]{:S(2)}) collective-permute-start(bf16[128,2048]{1,0:T(8,128)(2,1)S(1)} %get-tuple-element.28), channel_id=1, source_target_pairs={{0,3},{1,0},{2,1},{3,2},{4,7},{5,4},{6,5},{7,6},{8,11},{9,8},{10,9... | collective-permute-start | bytes 1572872 | tf_op jit(solution)/shard_map/ppermute | solution.py:48
  127.7 3.8 %collective-permute-start.23 = (bf16[256,512]{1,0:T(8,128)(2,1)S(1)}, bf16[256,512]{1,0:T(8,128)(2,1)S(1)}, u32[]{:S(2)}, u32[]{:S(2)}) collective-permute-start(bf16[256,512]{1,0:T(8,128)(2,1)S(1)} %shard_map.85), channel_id=1, source_target_pairs={{0,4},{4,0},{8,12},{12,8},{16,20},{20,16},{24,28},{28,24},{32,36},... | collective-permute-start | bytes 786440 | tf_op jit(solution)/shard_map/ppermute | solution.py:44
  141.0 25.0 %collective-permute-start.27 = (bf16[128,4096]{1,0:T(8,128)(2,1)S(1)}, bf16[128,4096]{1,0:T(8,128)(2,1)S(1)}, u32[]{:S(2)}, u32[]{:S(2)}) collective-permute-start(bf16[128,4096]{1,0:T(8,128)(2,1)S(1)} %get-tuple-element.29), channel_id=1, source_target_pairs={{0,1},{1,2},{2,3},{3,0},{4,5},{5,6},{6,7},{7,4},{8,9},{9,10},{10,1... | collective-permute-start | bytes 3145736 | tf_op jit(solution)/shard_map/ppermute | solution.py:48
  141.1 24.9 %collective-permute-start.28 = (bf16[128,4096]{1,0:T(8,128)(2,1)S(1)}, bf16[128,4096]{1,0:T(8,128)(2,1)S(1)}, u32[]{:S(2)}, u32[]{:S(2)}) collective-permute-start(bf16[128,4096]{1,0:T(8,128)(2,1)S(1)} %get-tuple-element.30), channel_id=1, source_target_pairs={{0,3},{1,0},{2,1},{3,2},{4,7},{5,4},{6,5},{7,6},{8,11},{9,8},{10,9... | collective-permute-start | bytes 3145736 | tf_op jit(solution)/shard_map/ppermute | solution.py:48
  146.0 3.9 %collective-permute-start.22 = (bf16[128,512]{1,0:T(8,128)(2,1)S(1)}, bf16[128,512]{1,0:T(8,128)(2,1)S(1)}, u32[]{:S(2)}, u32[]{:S(2)}) collective-permute-start(bf16[128,512]{1,0:T(8,128)(2,1)S(1)} %shard_map.82), channel_id=1, source_target_pairs={{0,4},{4,0},{8,12},{12,8},{16,20},{20,16},{24,28},{28,24},{32,36},... | collective-permute-start | bytes 393224 | tf_op jit(solution)/shard_map/ppermute | solution.py:44
where the time goes:
time: 168 us; the launch traced here: 167 us
  waiting for transfers between devices  66.5 us (40%)
  starting transfers between devices  49.2 us (29%)
  Pallas kernels  43 us (26%)
  other arithmetic  5.19 us (3%)
  local copies, waits for them, and re-layouts  3.09 us (2%)
    ppermute x10, waiting for transfers between devices, send_tp(): return lax.ppermute(u, 'tp', tp_pairs(step))  38 us
    ppermute x6, waiting for transfers between devices, send_two(): return lax.ppermute(u, 'ctx', plane_pairs(step, False))  18.2 us
    pallas_call x6, Pallas kernels, attend(): pl.pallas_call(functools.partial(attend_kernel, side, offsets, len(arrays...  15.7 us
    ppermute x7, starting transfers between devices, core_swap(): return lax.ppermute(u, 'ctx', CORE_PAIRS)  15.2 us
    ppermute x10, starting transfers between devices, send_tp(): return lax.ppermute(u, 'tp', tp_pairs(step))  13.7 us
    ppermute x6, starting transfers between devices, send_two(): return lax.ppermute(u, 'ctx', plane_pairs(step, False))  11.2 us
    pallas_call x2, Pallas kernels, project_q(): pl.pallas_call(q_kernel, grid_spec=pltpu.PrefetchScalarGridSpec(num_scala...  9.85 us
    ppermute x6, starting transfers between devices, send_one(): return lax.ppermute(u, 'ctx', plane_pairs(step, True))  9.07 us
  transfers between devices with their start and end apart: 29, of which 11 were waited for; matrix products, arithmetic and copies ran while one was open for 2% of the time, Pallas kernels for 20%

commit v1 on v0

v1 whole, which is shorter than its diff:
```python
import functools

import jax
import jax.numpy as jnp
from jax import lax
from jax.experimental import pallas as pl
from jax.experimental.pallas import tpu as pltpu
from jax.sharding import PartitionSpec as P

HD = 128
BLK = 128
LIST = 8
ROPE_BASE = 500000.0
NEG_LARGE = -1e30
CHUNKS = 2
VMEM = 20 << 20
BF16 = jnp.bfloat16
F32 = jnp.float32


def ctx_index(z, y, c):
    return ((z % 4) * 4 + (y % 4)) * 2 + c


def plane_pairs(step, first):
    pairs = []
    for z in range(4):
        for y in range(4):
            for c in range(2):
                along_z = (c == 0) == first
                to = ctx_index(z + step, y, c) if along_z else ctx_index(z, y + step, c)
                pairs.append((ctx_index(z, y, c), to))
    return pairs


CORE_PAIRS = [(i, i ^ 1) for i in range(32)]


def tp_pairs(step):
    return [
        (i * 4 + t, i * 4 + (t + (step if i % 2 == 0 else -step)) % 4) for i in range(32) for t in range(4)
    ]


def cost(us):
    return pl.CostEstimate(flops=int(us * 1.1e9), bytes_accessed=0, transcendentals=0)


def core_swap(u):
    return lax.ppermute(u, "ctx", CORE_PAIRS)


def send_tp(u, step):
    return lax.ppermute(u, ("ctx", "tp"), tp_pairs(step))


def send_one(u, step):
    return lax.ppermute(u, "ctx", plane_pairs(step, True))


def send_two(u, step):
    return lax.ppermute(u, "ctx", plane_pairs(step, False))


def roped(u, cosine, sine):
    return u * cosine + pltpu.roll(u, HD // 2, 1) * sine


def kv_part_kernel(n, ids, *refs):
    sources, (wk, wv, tk, tv) = refs[:n], refs[n:]
    step = pl.program_id(0)
    for at, ref in enumerate(sources):

        @pl.when(step == at)
        def _(at=at, ref=ref):
            for w, total in ((wk, tk), (wv, tv)):
                part = jnp.dot(ref[...], w[...], preferred_element_type=F32)
                if at == 0:
                    total[...] = part
                else:
                    total[...] += part


def kv_part(ids, sources, wk, wv):
    n = len(sources)
    rows, depth = sources[0].shape
    whole = pl.BlockSpec((rows, depth), lambda k, ids: (0, 0))
    w_spec = pl.BlockSpec((depth, 2 * HD), lambda k, ids: (ids[k], 0))
    out = jax.ShapeDtypeStruct((rows, 2 * HD), F32)
    return pl.pallas_call(
        functools.partial(kv_part_kernel, n),
        grid_spec=pltpu.PrefetchScalarGridSpec(
            num_scalar_prefetch=1,
            grid=(n,),
            in_specs=[whole] * n + [w_spec, w_spec],
            out_specs=[pl.BlockSpec((rows, 2 * HD), lambda k, ids: (0, 0))] * 2,
        ),
        out_shape=[out, out],
        compiler_params=pltpu.CompilerParams(vmem_limit_bytes=VMEM),
        cost_estimate=cost(len(sources)),
    )(ids, *sources, wk, wv)


def kv_kernel(ids, far, wk, wv, pk, pv, cos, sin, mine, theirs):
    keys = pk[...] + jnp.dot(far[...], wk[...], preferred_element_type=F32)
    vals = pv[...] + jnp.dot(far[...], wv[...], preferred_element_type=F32)
    cosine, sine = cos[...], sin[...]
    keys = [roped(keys[:, h * HD : (h + 1) * HD], cosine, sine).astype(BF16) for h in range(2)]
    vals = [vals[:, h * HD : (h + 1) * HD].astype(BF16) for h in range(2)]

    for core in range(2):

        @pl.when(ids[4] == core)
        def _(core=core):
            mine[:, :HD] = keys[core]
            mine[:, HD:] = vals[core]
            theirs[:, :HD] = keys[1 - core]
            theirs[:, HD:] = vals[1 - core]


def project_kv(ids, chunk, far, parts, wk, wv, cos, sin):
    rows, depth = far.shape
    whole = lambda shape: pl.BlockSpec(shape, lambda k, ids: (0, 0))
    w_spec = pl.BlockSpec((depth, 2 * HD), lambda k, ids: (ids[3], 0))
    table = pl.BlockSpec((rows, HD), lambda k, ids: (chunk, 0))
    out = jax.ShapeDtypeStruct((rows, 2 * HD), BF16)
    return pl.pallas_call(
        kv_kernel,
        grid_spec=pltpu.PrefetchScalarGridSpec(
            num_scalar_prefetch=1,
            grid=(1,),
            in_specs=[whole(far.shape), w_spec, w_spec, whole((rows, 2 * HD)), whole((rows, 2 * HD)), table, table],
            out_specs=[whole((rows, 2 * HD))] * 2,
        ),
        out_shape=[out, out],
        compiler_params=pltpu.CompilerParams(vmem_limit_bytes=VMEM),
        cost_estimate=cost(1),
    )(ids, far, wk, wv, *parts, cos, sin)


def q_kernel(ids, *refs):
    parts, (wq, cos, sin, out) = [refs[4 * k : 4 * k + 4] for k in range(CHUNKS)], refs[4 * CHUNKS :]
    depth = parts[0][0].shape[1]
    at = [pl.ds(pl.multiple_of(ids[k] * depth, depth), depth) for k in range(4)]
    for chunk, sources in enumerate(parts):
        rows = sources[0].shape[0]
        span = slice(chunk * rows, (chunk + 1) * rows)
        total = sum(jnp.dot(sources[k][...], wq[at[k], :], preferred_element_type=F32) for k in range(4))
        cosine, sine = cos[span, :], sin[span, :]
        for h in range(2):
            turned = roped(total[:, h * HD : (h + 1) * HD], cosine, sine) * HD ** (-0.5)
            out[span, h * HD : (h + 1) * HD] = turned.astype(BF16)


def project_q(ids, side, sources, wq, cos, sin):
    rows, inner = cos.shape[0], wq.shape[0]
    flat = [u for part in sources for u in part]
    whole = lambda u: pl.BlockSpec(u.shape, lambda j, ids: (0, 0))
    return pl.pallas_call(
        q_kernel,
        grid_spec=pltpu.PrefetchScalarGridSpec(
            num_scalar_prefetch=1,
            grid=(2,),
            in_specs=[whole(u) for u in flat]
            + [
                pl.BlockSpec((inner, 2 * HD), lambda j, ids: (0, 2 * ids[4 + side] + j)),
                whole(cos),
                whole(sin),
            ],
            out_specs=pl.BlockSpec((rows, 2 * HD), lambda j, ids: (0, j)),
        ),
        out_shape=jax.ShapeDtypeStruct((rows, 4 * HD), BF16),
        compiler_params=pltpu.CompilerParams(vmem_limit_bytes=VMEM),
        cost_estimate=cost(5),
    )(ids, *flat, wq, cos, sin)


def pack_kernel(*refs):
    parts, out = refs[:-1], refs[-1]
    rows = parts[0].shape[0]
    for k, u in enumerate(parts):
        out[k * rows : (k + 1) * rows, :] = u[...]


def pack(*parts):
    rows, cols = parts[0].shape
    vmem = pl.BlockSpec(memory_space=pltpu.VMEM)
    return pl.pallas_call(
        pack_kernel,
        in_specs=[vmem] * len(parts),
        out_specs=vmem,
        out_shape=jax.ShapeDtypeStruct((len(parts) * rows, cols), parts[0].dtype),
        compiler_params=pltpu.CompilerParams(vmem_limit_bytes=VMEM),
        cost_estimate=cost(0.4),
    )(*parts)


def attend_kernel(side, steps, n_arrays, ids, table, lengths, query, *rest):
    arrays, (out, held) = rest[:n_arrays], rest[n_arrays:]
    turned = 1 - 2 * ids[4 + side]
    blocks = [lax.rem(ids[0] + 4 + step * turned, 4) for step in steps]

    for n, block in enumerate(blocks):
        for e in range(LIST):
            place = table[(side * 4 + block) * LIST + e]
            to = slice((n * LIST + e) * BLK, (n * LIST + e + 1) * BLK)

            def from_array(ref, place=place, to=to):
                def go():
                    held[to, :] = ref[pl.ds(pl.multiple_of(lax.rem(place, 64) * BLK, BLK), BLK), :]

                return go

            lax.switch(lax.div(place, 64), [from_array(r) for r in arrays])

    rows = lax.broadcasted_iota(jnp.int32, (BLK, BLK), 0)
    lanes = lax.broadcasted_iota(jnp.int32, (BLK, BLK), 1)
    for n, block in enumerate(blocks):
        at = pl.ds(pl.multiple_of(block * BLK, BLK), BLK)
        position = rows + (ids[6 + side] + block * BLK)
        begin, end = jnp.zeros_like(rows), 0
        for d in range(lengths.shape[0]):
            end = end + lengths[d]
            begin = jnp.where(position >= end, end, begin)
        bias = []
        for e in range(LIST):
            index = lanes + table[(8 + side * 4 + block) * LIST + e]
            bias.append(jnp.where((index <= position) & (index >= begin), 0.0, NEG_LARGE))
        bias = jnp.concatenate(bias, axis=1)
        span = slice(n * LIST * BLK, (n + 1) * LIST * BLK)
        keys = held[span, :HD]
        values = held[span, HD:]
        part = jnp.concatenate([query[at, h * HD : (h + 1) * HD] for h in range(4)])
        scores = lax.dot_general(part, keys, (((1,), (1,)), ((), ())), preferred_element_type=F32)
        rounded, totals = [], []
        for h in range(4):
            masked = scores[h * BLK : (h + 1) * BLK] + bias
            weights = jnp.exp(masked - jnp.max(masked, axis=1, keepdims=True))
            totals.append(jnp.sum(weights, axis=1, keepdims=True))
            rounded.append(weights.astype(BF16))
        mixed = jnp.dot(jnp.concatenate(rounded), values, preferred_element_type=F32)
        for h in range(4):
            done = mixed[h * BLK : (h + 1) * BLK] / totals[h]
            out[n * BLK : (n + 1) * BLK, h * HD : (h + 1) * HD] = done.astype(BF16)


def attend(side, steps, ids, table, lengths, query, arrays):
    count = len(steps)
    smem = pl.BlockSpec(memory_space=pltpu.SMEM)
    vmem = pl.BlockSpec(memory_space=pltpu.VMEM)
    return pl.pallas_call(
        functools.partial(attend_kernel, side, steps, len(arrays)),
        in_specs=[smem] * 3 + [vmem] * (1 + len(arrays)),
        out_specs=vmem,
        out_shape=jax.ShapeDtypeStruct((count * BLK, 4 * HD), BF16),
        scratch_shapes=[pltpu.VMEM((count * LIST * BLK, 2 * HD), BF16)],
        compiler_params=pltpu.CompilerParams(vmem_limit_bytes=VMEM),
        cost_estimate=cost(1 + 1.2 * count),
    )(ids, table, lengths, query, *arrays)


def heads_in_order(core, mine, other):
    return jnp.concatenate(
        [jnp.where(core == 0, mine, other), jnp.where(core == 0, other, mine)], axis=1
    )


TILE = 512


def out_kernel(core, mine, other, w, *outs):
    rows = heads_in_order(core[0], mine[...], other[...])
    part = jnp.dot(rows, w[...], preferred_element_type=F32)
    for k, out in enumerate(outs):
        out[...] = part[k * BLK : (k + 1) * BLK].astype(out.dtype)


def project_out(core, mine, other, wo, types):
    cols = wo.shape[1]
    whole = pl.BlockSpec(mine.shape, lambda j, core: (0, 0))
    return pl.pallas_call(
        out_kernel,
        grid_spec=pltpu.PrefetchScalarGridSpec(
            num_scalar_prefetch=1,
            grid=(cols // TILE,),
            in_specs=[whole, whole, pl.BlockSpec((wo.shape[0], TILE), lambda j, core: (0, j))],
            out_specs=[pl.BlockSpec((BLK, TILE), lambda j, core: (0, j))] * len(types),
        ),
        out_shape=[jax.ShapeDtypeStruct((BLK, cols), t) for t in types],
        compiler_params=pltpu.CompilerParams(vmem_limit_bytes=VMEM),
        cost_estimate=cost(2 + len(types)),
    )(core, mine, other, wo)


def rope_tables(positions):
    frequency = ROPE_BASE ** (-(jnp.arange(HD // 2, dtype=F32) * 2.0 / HD))
    angles = positions.astype(F32)[:, None] * frequency[None, :]
    cosine, sine = jnp.cos(angles), jnp.sin(angles)
    return jnp.concatenate([cosine, cosine], axis=1), jnp.concatenate([-sine, sine], axis=1)


def fresh_entries(pattern):
    equal = pattern[:, :, None] == pattern[:, None, :]
    earlier = jnp.tril(jnp.ones((LIST, LIST), dtype=bool), -1)
    return jnp.logical_not(jnp.any(equal & earlier[None], axis=2))


def block_places(pattern, me):
    core, y, z = me % 2, (me // 2) % 4, me // 8
    per = 4 // CHUNKS
    chip = pattern // 8
    from_z, from_y = chip // 4, chip % 4
    other, local = ((pattern // 4) % 2 != core).astype(jnp.int32), pattern % 4
    along_one = jnp.where(core == 0, z - from_z, y - from_y) % 4
    along_two = jnp.where(core == 0, y - from_y, z - from_z) % 4
    slots = [jnp.where(u == 3, 2, jnp.where(u == 2, 3, u)) for u in (along_one, along_two)]
    array = (local // per) * 4 + slots[1]
    return array * 64 + (slots[0] * 2 + other) * per + local % per


def after(u, *others):
    return lax.optimization_barrier((u, *others))[0]


def on_device(x_tokens, w_query, w_key, w_value, w_output, pattern, doc_lengths):
    rows = x_tokens.shape[0]
    tp, me = lax.axis_index("tp"), lax.axis_index("ctx")
    core = me % 2
    length = rows // CHUNKS
    ids = jnp.stack(
        [tp, (tp + 3 + 2 * core) % 4, (tp + 1 + 2 * core) % 4, (tp + 2) % 4, core, 1 - core, me * rows, (me ^ 1) * rows]
    ).astype(jnp.int32)
    cos, sin = rope_tables(me * rows + jnp.arange(rows, dtype=jnp.int32))
    listed = jnp.concatenate([pattern, core_swap(pattern)])
    base = jnp.where(fresh_entries(listed), listed * BLK, 1 << 24)
    table = jnp.concatenate([block_places(listed, me), base]).astype(jnp.int32).reshape(-1)

    first, second = x_tokens[:length], x_tokens[length:]
    first_before, first_after = send_tp(first, 1), send_tp(first, -1)
    first_far = send_tp(after(first_before, ids, cos, sin, table), 1)
    second_before = send_tp(after(second, first_before, first_after), 1)
    second_after = send_tp(after(second, first_before, first_after), -1)
    parts = kv_part(ids, (first, first_before, first_after), w_key, w_value)
    mine, theirs = project_kv(ids, 0, first_far, parts, w_key, w_value, cos, sin)
    second_far = send_tp(after(second_before, theirs), 1)
    sources = [
        (first, first_before, first_after, first_far),
        (second, second_before, second_after, second_far),
    ]
    gathered = []
    for chunk in range(CHUNKS):
        if chunk:
            held = after(second, line)
            parts = kv_part(ids, (held, second_before, second_after), w_key, w_value)
            mine, theirs = project_kv(ids, 1, second_far, parts, w_key, w_value, cos, sin)
        shard = pack(mine, core_swap(theirs))
        line = pack(shard, *[send_one(shard, step) for step in (1, -1, 2)])
        near = {step: send_two(line, step) for step in (1, -1)}
        way = 1 - 2 * chunk
        onward = near[way]
        if chunk:
            query = [project_q(ids, side, sources, w_query, cos, sin) for side in (0, 1)]
            onward = after(onward, *query)
        gathered += [line, near[1], near[-1], send_two(onward, way)]
    query[1] = core_swap(query[1])

    def attended(*steps):
        other = core_swap(attend(1, steps, ids, table, doc_lengths, query[1], gathered))
        return attend(0, steps, ids, table, doc_lengths, query[0], gathered), other

    core_id = ids[4:5]
    (far,) = project_out(core_id, *attended(2), w_output, (BF16,))
    arrived = send_tp(far, 1)
    ahead, behind = project_out(core_id, *attended(1, -1), w_output, (F32, BF16))
    from_after = send_tp(behind, -1)
    from_before = send_tp((ahead + arrived.astype(F32)).astype(BF16), 1)
    (own,) = project_out(core_id, *attended(0), w_output, (F32,))
    return (own + from_before.astype(F32) + from_after.astype(F32)).astype(BF16)


def solution(mesh):
    return jax.shard_map(
        on_device,
        mesh=mesh,
        in_specs=(
            P("ctx", "tp"),
            P(None, "tp"),
            P(None, "tp"),
            P(None, "tp"),
            P("tp", None),
            P("ctx", None),
            P(),
        ),
        out_specs=P(("ctx", "tp"), None),
        check_vma=False,
    )
```

time: 168 us -> 160 us (0.952)
  waiting for transfers between devices: 66.5 us -> 60.9 us
  starting transfers between devices: 49.2 us -> 45.9 us
  Pallas kernels: 43 us -> 45.2 us
  other arithmetic: 5.19 us -> 3.29 us
    ppermute x10 -> x9, waiting for transfers between devices: 38 us -> 28.4 us  [send_tp(): return lax.ppermute(u, ('ctx', 'tp'), tp_pairs(step))]
    ppermute x7, starting transfers between devices: 15.2 us -> 21.7 us  [core_swap(): return lax.ppermute(u, 'ctx', CORE_PAIRS)]
    ppermute x6, starting transfers between devices: 11.2 us -> 4.96 us  [send_two(): return lax.ppermute(u, 'ctx', plane_pairs(step, False))]
    pallas_call x9 -> x11, Pallas kernels: 26.5 us -> 32.7 us  [the longest x6 16.2 us: attend(): pl.pallas_call(functools.partial(attend_kernel, side, steps, len(arrays))...]
    ppermute x6, waiting for transfers between devices: 7.81 us -> 12.8 us  [send_one(): return lax.ppermute(u, 'ctx', plane_pairs(step, True))]
    pallas_call x2, Pallas kernels: 6.52 us -> 2.19 us  [project_kv(): pl.pallas_call(kv_kernel, grid_spec=pltpu.PrefetchScalarGridSpec(num_scal...]
    ppermute x10 -> x9, starting transfers between devices: 13.7 us -> 10.4 us  [send_tp(): return lax.ppermute(u, ('ctx', 'tp'), tp_pairs(step))]
    ppermute x6, waiting for transfers between devices: 18.2 us -> 16.2 us  [send_two(): return lax.ppermute(u, 'ctx', plane_pairs(step, False))]
  transfers between devices with their start and end apart: 29 -> 28, of which waited for: 11 -> 19; matrix products, arithmetic and copies ran while one was open for 2% -> 1% of each run, Pallas kernels for 20% -> 24%
where the time goes in v1:
time: 160 us
  waiting for transfers between devices  60.9 us (38%)
  starting transfers between devices  45.9 us (29%)
  Pallas kernels  45.2 us (28%)
  local copies, waits for them, and re-layouts  4.01 us (3%)
  other arithmetic  3.29 us (2%)
    ppermute x9, waiting for transfers between devices, send_tp(): return lax.ppermute(u, ('ctx', 'tp'), tp_pairs(step))  28.4 us
    ppermute x7, starting transfers between devices, core_swap(): return lax.ppermute(u, 'ctx', CORE_PAIRS)  21.7 us
    pallas_call x6, Pallas kernels, attend(): pl.pallas_call(functools.partial(attend_kernel, side, steps, len(arrays))...  16.2 us
    ppermute x6, waiting for transfers between devices, send_two(): return lax.ppermute(u, 'ctx', plane_pairs(step, False))  16.2 us
    ppermute x6, waiting for transfers between devices, send_one(): return lax.ppermute(u, 'ctx', plane_pairs(step, True))  12.8 us
    pallas_call x3, Pallas kernels, project_out(): pl.pallas_call(out_kernel, grid_spec=pltpu.PrefetchScalarGridSpec(num_sca...  11.2 us
    ppermute x9, starting transfers between devices, send_tp(): return lax.ppermute(u, ('ctx', 'tp'), tp_pairs(step))  10.4 us
    pallas_call x2, Pallas kernels, project_q(): pl.pallas_call(q_kernel, grid_spec=pltpu.PrefetchScalarGridSpec(num_scala...  10.2 us
  transfers between devices with their start and end apart: 28, of which 19 were waited for; matrix products, arithmetic and copies ran while one was open for 1% of the time, Pallas kernels for 24%

profile of v1, /device:TPU:1, one launch (start us, length us, event | category | flops | bytes accessed | tf_op | source)
XLA Modules:
  0.0 159.7 jit_solution(13749141927036301013)
XLA Ops:
  0.0 2.2 %fusion.27 = (bf16[256,1024]{1,0:T(8,128)(2,1)S(1)}, bf16[256,1024]{1,0:T(8,128)(2,1)}) fusion(bf16[512,1024]{1,0:T(8,128)(2,1)} %param.7), kind=kLoop, calls=%fused_computation.73 | loop fusion | bytes 2097152 | tf_op jit(solution)/shard_map/slice | solution.py:338
  2.2 2.0 %collective-permute-start.2 = (bf16[256,1024]{1,0:T(8,128)(2,1)}, bf16[256,1024]{1,0:T(8,128)(2,1)}, u32[]{:S(2)}, u32[]{:S(2)}) collective-permute-start(bf16[256,1024]{1,0:T(8,128)(2,1)} %get-tuple-element.36.refs_0_), channel_id=1, source_target_pairs={{0,3},{1,0},{2,1},{3,2},{4,5},{5,6},{6,7},{7,4},{8,11},{9,8},{10,9... | collective-permute-start | bytes 1572872 | tf_op jit(solution)/shard_map/ppermute | solution.py:54
  4.3 1.3 collective-permute-start.1
  5.5 1.0 collective-permute-start
  6.6 1.0 fusion
  7.9 0.3 and_reduce_fusion
  8.3 10.0 %collective-permute-done.1.refs_1_ = bf16[256,1024]{1,0:T(8,128)(2,1)} collective-permute-done((bf16[256,1024]{1,0:T(8,128)(2,1)}, bf16[256,1024]{1,0:T(8,128)(2,1)}, u32[]{:S(2)}, u32[]{:S(2)}) %collective-permute-start.1) | collective-permute-done | bytes 524320 | tf_op jit(solution)/shard_map/ppermute | solution.py:54
  18.3 1.5 collective-permute-start.3
  19.9 2.7 %collective-permute-start.4 = (bf16[256,1024]{1,0:T(8,128)(2,1)S(1)}, bf16[256,1024]{1,0:T(8,128)(2,1)S(1)}, u32[]{:S(2)}, u32[]{:S(2)}) collective-permute-start(bf16[256,1024]{1,0:T(8,128)(2,1)S(1)} %get-tuple-element.27.refs_4_.refs_0_), channel_id=1, source_target_pairs={{0,1},{1,2},{2,3},{3,0},{4,7},{5,4},{6,5},{7,6},{8,9},{9,10},{10,1... | collective-permute-start | bytes 1572872 | tf_op jit(solution)/shard_map/ppermute | solution.py:54
  22.5 1.6 copy-done.1
  24.1 3.3 %shard_map.73 = (f32[256,256]{1,0:T(8,128)S(1)}, f32[256,256]{1,0:T(8,128)S(1)}) custom-call(s32[8]{0:T(128)S(1)} %stack.35.ids, bf16[256,1024]{1,0:T(8,128)(2,1)} %get-tuple-element.36.refs_0_, bf16[256,1024]{1,0:T(8,128)(2,1)} %collective-permute-done.1.refs_1_, bf16[256,1024]{1,0:T(8,128)(2,1)} %collective-permute-done.2.refs_2_, ...), custom_call_target="tpu_custom_call" | custom-call | flops 3300000000 | tf_op jit(solution)/shard_map/pallas_call | solution.py:90
  27.5 3.9 %collective-permute-done.3.far.refs_3_ = bf16[256,1024]{1,0:T(8,128)(2,1)S(1)} collective-permute-done((bf16[256,1024]{1,0:T(8,128)(2,1)}, bf16[256,1024]{1,0:T(8,128)(2,1)S(1)}, u32[]{:S(2)}, u32[]{:S(2)}) %collective-permute-start.3) | collective-permute-done | bytes 524320 | tf_op jit(solution)/shard_map/ppermute | solution.py:54
  31.3 1.1 shard_map.74
  32.4 3.3 %collective-permute-start.7 = (bf16[256,256]{1,0:T(8,128)(2,1)S(1)}, bf16[256,256]{1,0:T(8,128)(2,1)S(1)}, u32[]{:S(2)}, u32[]{:S(2)}) collective-permute-start(bf16[256,256]{1,0:T(8,128)(2,1)S(1)} %get-tuple-element.24), channel_id=1, source_target_pairs={{0,4},{4,0},{8,12},{12,8},{16,20},{20,16},{24,28},{28,24},{32,36},... | collective-permute-start | bytes 393224 | tf_op jit(solution)/shard_map/ppermute | solution.py:50
  35.7 1.0 collective-permute-done.7.refs_1_
  36.7 2.9 %collective-permute-start.10 = (bf16[512,256]{1,0:T(8,128)(2,1)S(1)}, bf16[512,256]{1,0:T(8,128)(2,1)S(1)}, u32[]{:S(2)}, u32[]{:S(2)}) collective-permute-start(bf16[512,256]{1,0:T(8,128)(2,1)S(1)} %shard_map.76.refs_0_), channel_id=1, source_target_pairs={{0,64},{4,20},{8,72},{12,28},{16,80},{20,4},{24,88},{28,12},{32,96... | collective-permute-start | bytes 786440 | tf_op jit(solution)/shard_map/ppermute | solution.py:58
  39.7 0.8 collective-permute-start.9
  40.4 0.7 collective-permute-start.8
  41.1 0.5 collective-permute-start.6
  41.7 2.2 %collective-permute-done.10.refs_3_ = bf16[512,256]{1,0:T(8,128)(2,1)S(1)} collective-permute-done((bf16[512,256]{1,0:T(8,128)(2,1)S(1)}, bf16[512,256]{1,0:T(8,128)(2,1)S(1)}, u32[]{:S(2)}, u32[]{:S(2)}) %collective-permute-start.10) | collective-permute-done | bytes 262176 | tf_op jit(solution)/shard_map/ppermute | solution.py:58
  43.8 3.1 %collective-permute-done.9.refs_2_ = bf16[512,256]{1,0:T(8,128)(2,1)S(1)} collective-permute-done((bf16[512,256]{1,0:T(8,128)(2,1)S(1)}, bf16[512,256]{1,0:T(8,128)(2,1)S(1)}, u32[]{:S(2)}, u32[]{:S(2)}) %collective-permute-start.9) | collective-permute-done | bytes 262176 | tf_op jit(solution)/shard_map/ppermute | solution.py:58
  47.3 2.0 %shard_map.78 = (f32[256,256]{1,0:T(8,128)S(1)}, f32[256,256]{1,0:T(8,128)S(1)}) custom-call(s32[8]{0:T(128)S(1)} %stack.35.ids, bf16[256,1024]{1,0:T(8,128)(2,1)S(1)} %get-tuple-element.27.refs_4_.refs_0_, bf16[256,1024]{1,0:T(8,128)(2,1)S(1)} %collective-permute-done.4.refs_5_.refs_1_, bf16[256,1024]{1,0:T(8,128)(2,1)S(1)} %collective-permute-done.5.refs_6_.refs_2_, ...), custom_call_target="tpu_custom_call" | custom-call | flops 3300000000 | tf_op jit(solution)/shard_map/pallas_call | solution.py:90
  49.2 0.2 collective-permute-done.6.refs_7_.far
  49.5 1.1 shard_map.79
  50.6 4.0 %collective-permute-start.14 = (bf16[256,256]{1,0:T(8,128)(2,1)S(1)}, bf16[256,256]{1,0:T(8,128)(2,1)S(1)}, u32[]{:S(2)}, u32[]{:S(2)}) collective-permute-start(bf16[256,256]{1,0:T(8,128)(2,1)S(1)} %get-tuple-element.31), channel_id=1, source_target_pairs={{0,4},{4,0},{8,12},{12,8},{16,20},{20,16},{24,28},{28,24},{32,36},... | collective-permute-start | bytes 393224 | tf_op jit(solution)/shard_map/ppermute | solution.py:50
  54.6 1.0 collective-permute-done.14.refs_1_
  55.6 3.0 %collective-permute-start.17 = (bf16[512,256]{1,0:T(8,128)(2,1)S(1)}, bf16[512,256]{1,0:T(8,128)(2,1)S(1)}, u32[]{:S(2)}, u32[]{:S(2)}) collective-permute-start(bf16[512,256]{1,0:T(8,128)(2,1)S(1)} %shard_map.80.refs_0_), channel_id=1, source_target_pairs={{0,64},{4,20},{8,72},{12,28},{16,80},{20,4},{24,88},{28,12},{32,96... | collective-permute-start | bytes 786440 | tf_op jit(solution)/shard_map/ppermute | solution.py:58
  58.6 0.8 collective-permute-start.16
  59.4 0.7 collective-permute-start.15
  60.1 0.7 collective-permute-start.11
  60.8 1.9 %collective-permute-done.17.refs_3_ = bf16[512,256]{1,0:T(8,128)(2,1)S(1)} collective-permute-done((bf16[512,256]{1,0:T(8,128)(2,1)S(1)}, bf16[512,256]{1,0:T(8,128)(2,1)S(1)}, u32[]{:S(2)}, u32[]{:S(2)}) %collective-permute-start.17) | collective-permute-done | bytes 262176 | tf_op jit(solution)/shard_map/ppermute | solution.py:58
  62.7 3.2 %collective-permute-done.16.refs_2_ = bf16[512,256]{1,0:T(8,128)(2,1)S(1)} collective-permute-done((bf16[512,256]{1,0:T(8,128)(2,1)S(1)}, bf16[512,256]{1,0:T(8,128)(2,1)S(1)}, u32[]{:S(2)}, u32[]{:S(2)}) %collective-permute-start.16) | collective-permute-done | bytes 262176 | tf_op jit(solution)/shard_map/ppermute | solution.py:58
  65.9 2.2 %collective-permute-done.15.refs_1_ = bf16[512,256]{1,0:T(8,128)(2,1)S(1)} collective-permute-done((bf16[512,256]{1,0:T(8,128)(2,1)S(1)}, bf16[512,256]{1,0:T(8,128)(2,1)S(1)}, u32[]{:S(2)}, u32[]{:S(2)}) %collective-permute-start.15) | collective-permute-done | bytes 262176 | tf_op jit(solution)/shard_map/ppermute | solution.py:58
  68.2 0.3 collective-permute-start.19
  68.5 1.1 collective-permute-start.12
  69.6 5.1 %shard_map.75.query = bf16[512,512]{1,0:T(8,128)(2,1)S(1)} custom-call(s32[8]{0:T(128)S(1)} %stack.35.ids, bf16[256,1024]{1,0:T(8,128)(2,1)} %get-tuple-element.36.refs_0_, bf16[256,1024]{1,0:T(8,128)(2,1)} %collective-permute-done.1.refs_1_, bf16[256,1024]{1,0:T(8,128)(2,1)} %collective-permute-done.2.refs_2_, ...), custom_call_target="tpu_custom_call" | custom-call | flops 5500000256 | tf_op jit(solution)/shard_map/pallas_call | solution.py:159
  74.7 5.1 %shard_map.82 = bf16[512,512]{1,0:T(8,128)(2,1)S(1)} custom-call(s32[8]{0:T(128)S(1)} %stack.35.ids, bf16[256,1024]{1,0:T(8,128)(2,1)} %get-tuple-element.36.refs_0_, bf16[256,1024]{1,0:T(8,128)(2,1)} %collective-permute-done.1.refs_1_, bf16[256,1024]{1,0:T(8,128)(2,1)} %collective-permute-done.2.refs_2_, ...), custom_call_target="tpu_custom_call" | custom-call | flops 5500000256 | tf_op jit(solution)/shard_map/pallas_call | solution.py:159
  79.8 0.5 collective-permute-start.18
  80.3 1.2 collective-permute-start.13
  81.5 0.7 collective-permute-done.19.rest_6_
  82.2 1.2 collective-permute-start.20
  83.4 5.9 %collective-permute-start.21 = (bf16[512,512]{1,0:T(8,128)(2,1)S(1)}, bf16[512,512]{1,0:T(8,128)(2,1)S(1)}, u32[]{:S(2)}, u32[]{:S(2)}) collective-permute-start(bf16[512,512]{1,0:T(8,128)(2,1)S(1)} %shard_map.82), channel_id=1, source_target_pairs={{0,4},{4,0},{8,12},{12,8},{16,20},{20,16},{24,28},{28,24},{32,36},... | collective-permute-start | bytes 1572872 | tf_op jit(solution)/shard_map/ppermute | solution.py:50
  89.3 1.5 collective-permute-done.21.query
  90.8 2.6 %collective-permute-done.12.rest_2_ = bf16[2048,256]{1,0:T(8,128)(2,1)S(1)} collective-permute-done((bf16[2048,256]{1,0:T(8,128)(2,1)S(1)}, bf16[2048,256]{1,0:T(8,128)(2,1)S(1)}, u32[]{:S(2)}, u32[]{:S(2)}) %collective-permute-start.12) | collective-permute-done | bytes 1048608 | tf_op jit(solution)/shard_map/ppermute | solution.py:62
  93.4 1.6 collective-permute-done.18.rest_5_
  95.0 11.2 %collective-permute-done.13.rest_3_ = bf16[2048,256]{1,0:T(8,128)(2,1)S(1)} collective-permute-done((bf16[2048,256]{1,0:T(8,128)(2,1)S(1)}, bf16[2048,256]{1,0:T(8,128)(2,1)S(1)}, u32[]{:S(2)}, u32[]{:S(2)}) %collective-permute-start.13) | collective-permute-done | bytes 1048608 | tf_op jit(solution)/shard_map/ppermute | solution.py:62
  106.2 2.3 %shard_map.90 = bf16[128,512]{1,0:T(8,128)(2,1)S(1)} custom-call(s32[8]{0:T(128)S(1)} %stack.35.ids, s32[128]{0:T(128)S(1)} %reshape.29.table, s32[16]{0:T(128)S(1)} %copy-done.2, bf16[512,512]{1,0:T(8,128)(2,1)S(1)} %collective-permute-done.21.query, bf16[2048,256]{1,0:T(8,128)(2,1)S(1)} %shard_map.77.rest_0_, ...), custom_call_target="tpu_custom_call" | custom-call | flops 2420000000 | tf_op jit(solution)/shard_map/pallas_call | solution.py:251
  108.6 6.0 %collective-permute-start.24 = (bf16[128,512]{1,0:T(8,128)(2,1)S(1)}, bf16[128,512]{1,0:T(8,128)(2,1)S(1)}, u32[]{:S(2)}, u32[]{:S(2)}) collective-permute-start(bf16[128,512]{1,0:T(8,128)(2,1)S(1)} %shard_map.90), channel_id=1, source_target_pairs={{0,4},{4,0},{8,12},{12,8},{16,20},{20,16},{24,28},{28,24},{32,36},... | collective-permute-start | bytes 393224 | tf_op jit(solution)/shard_map/ppermute | solution.py:50
  114.6 2.4 %shard_map.89.mine = bf16[128,512]{1,0:T(8,128)(2,1)S(1)} custom-call(s32[8]{0:T(128)S(1)} %stack.35.ids, s32[128]{0:T(128)S(1)} %reshape.29.table, s32[16]{0:T(128)S(1)} %copy-done.2, bf16[512,512]{1,0:T(8,128)(2,1)S(1)} %shard_map.75.query, bf16[2048,256]{1,0:T(8,128)(2,1)S(1)} %shard_map.77.rest_0_, ...), custom_call_target="tpu_custom_call" | custom-call | flops 2420000000 | tf_op jit(solution)/shard_map/pallas_call | solution.py:251
  117.1 3.3 %shard_map.91 = bf16[128,4096]{1,0:T(8,128)(2,1)S(1)} custom-call(s32[1]{0:T(128)} %bitcast.core, bf16[128,512]{1,0:T(8,128)(2,1)S(1)} %shard_map.89.mine, bf16[128,512]{1,0:T(8,128)(2,1)S(1)} %collective-permute-done.24.other, bf16[1024,4096]{1,0:T(8,128)(2,1)S(1)} %bitcast.11), custom_call_target="tpu_custom_call" | custom-call | flops 3300000000 | tf_op jit(solution)/shard_map/pallas_call | solution.py:281
  120.5 3.5 %shard_map.87 = bf16[256,512]{1,0:T(8,128)(2,1)S(1)} custom-call(s32[8]{0:T(128)S(1)} %stack.35.ids, s32[128]{0:T(128)S(1)} %reshape.29.table, s32[16]{0:T(128)S(1)} %copy-done.2, bf16[512,512]{1,0:T(8,128)(2,1)S(1)} %collective-permute-done.21.query, bf16[2048,256]{1,0:T(8,128)(2,1)S(1)} %shard_map.77.rest_0_, ...), custom_call_target="tpu_custom_call" | custom-call | flops 3740000000 | tf_op jit(solution)/shard_map/pallas_call | solution.py:251
  124.2 3.4 %shard_map.86.mine = bf16[256,512]{1,0:T(8,128)(2,1)S(1)} custom-call(s32[8]{0:T(128)S(1)} %stack.35.ids, s32[128]{0:T(128)S(1)} %reshape.29.table, s32[16]{0:T(128)S(1)} %copy-done.2, bf16[512,512]{1,0:T(8,128)(2,1)S(1)} %shard_map.75.query, bf16[2048,256]{1,0:T(8,128)(2,1)S(1)} %shard_map.77.rest_0_, ...), custom_call_target="tpu_custom_call" | custom-call | flops 3740000000 | tf_op jit(solution)/shard_map/pallas_call | solution.py:251
  127.6 4.5 %shard_map.88 = (f32[128,4096]{1,0:T(8,128)S(1)}, bf16[128,4096]{1,0:T(8,128)(2,1)S(1)}) custom-call(s32[1]{0:T(128)} %bitcast.core, bf16[256,512]{1,0:T(8,128)(2,1)S(1)} %shard_map.86.mine, bf16[256,512]{1,0:T(8,128)(2,1)S(1)} %collective-permute-done.23.other, bf16[1024,4096]{1,0:T(8,128)(2,1)S(1)} %bitcast.11), custom_call_target="tpu_custom_call" | custom-call | flops 4400000000 | tf_op jit(solution)/shard_map/pallas_call | solution.py:281
  132.1 1.4 collective-permute-start.27
  133.4 1.0 collective-permute-done.25
  134.4 0.3 add_convert_fusion.1
  134.7 1.0 collective-permute-start.26
  135.7 2.2 %shard_map.84 = bf16[128,512]{1,0:T(8,128)(2,1)S(1)} custom-call(s32[8]{0:T(128)S(1)} %stack.35.ids, s32[128]{0:T(128)S(1)} %reshape.29.table, s32[16]{0:T(128)S(1)} %copy-done.2, bf16[512,512]{1,0:T(8,128)(2,1)S(1)} %collective-permute-done.21.query, bf16[2048,256]{1,0:T(8,128)(2,1)S(1)} %shard_map.77.rest_0_, ...), custom_call_target="tpu_custom_call" | custom-call | flops 2420000000 | tf_op jit(solution)/shard_map/pallas_call | solution.py:251
  138.0 1.3 collective-permute-start.22
  139.2 2.3 %shard_map.83.mine = bf16[128,512]{1,0:T(8,128)(2,1)S(1)} custom-call(s32[8]{0:T(128)S(1)} %stack.35.ids, s32[128]{0:T(128)S(1)} %reshape.29.table, s32[16]{0:T(128)S(1)} %copy-done.2, bf16[512,512]{1,0:T(8,128)(2,1)S(1)} %shard_map.75.query, bf16[2048,256]{1,0:T(8,128)(2,1)S(1)} %shard_map.77.rest_0_, ...), custom_call_target="tpu_custom_call" | custom-call | flops 2420000000 | tf_op jit(solution)/shard_map/pallas_call | solution.py:251
  141.6 3.4 %shard_map.85 = f32[128,4096]{1,0:T(8,128)S(1)} custom-call(s32[1]{0:T(128)} %bitcast.core, bf16[128,512]{1,0:T(8,128)(2,1)S(1)} %shard_map.83.mine, bf16[128,512]{1,0:T(8,128)(2,1)S(1)} %collective-permute-done.22.other, bf16[1024,4096]{1,0:T(8,128)(2,1)S(1)} %bitcast.11), custom_call_target="tpu_custom_call" | custom-call | flops 3300000000 | tf_op jit(solution)/shard_map/pallas_call | solution.py:281
  144.9 8.8 %collective-permute-done.27 = bf16[128,4096]{1,0:T(8,128)(2,1)S(1)} collective-permute-done((bf16[128,4096]{1,0:T(8,128)(2,1)S(1)}, bf16[128,4096]{1,0:T(8,128)(2,1)S(1)}, u32[]{:S(2)}, u32[]{:S(2)}) %collective-permute-start.27) | collective-permute-done | bytes 1048608 | tf_op jit(solution)/shard_map/ppermute | solution.py:54
  153.7 4.6 %collective-permute-done.26 = bf16[128,4096]{1,0:T(8,128)(2,1)S(1)} collective-permute-done((bf16[128,4096]{1,0:T(8,128)(2,1)S(1)}, bf16[128,4096]{1,0:T(8,128)(2,1)S(1)}, u32[]{:S(2)}, u32[]{:S(2)}) %collective-permute-start.26) | collective-permute-done | bytes 1048608 | tf_op jit(solution)/shard_map/ppermute | solution.py:54
  158.3 1.4 add_convert_fusion
  (44 shorter events, 1.2 us)
Async XLA Ops:
  0.0 5.5 %copy-start.3 = (s32[4,8]{1,0:T(4,128)S(1)}, s32[4,8]{1,0:T(4,128)}, u32[]{:S(2)}) copy-start(s32[4,8]{1,0:T(4,128)} %param.12) | copy-start | bytes 388
  0.0 22.5 %copy-start = (bf16[4096,256]{1,0:T(8,128)(2,1)S(1)}, bf16[4096,256]{1,0:T(8,128)(2,1)}, u32[]{:S(2)}) copy-start(bf16[4096,256]{1,0:T(8,128)(2,1)} %wk.3) | copy-start | bytes 6291460
  2.2 17.6 %collective-permute-start.2 = (bf16[256,1024]{1,0:T(8,128)(2,1)}, bf16[256,1024]{1,0:T(8,128)(2,1)}, u32[]{:S(2)}, u32[]{:S(2)}) collective-permute-start(bf16[256,1024]{1,0:T(8,128)(2,1)} %get-tuple-element.36.refs_0_), channel_id=1, source_target_pairs={{0,3},{1,0},{2,1},{3,2},{4,5},{5,6},{6,7},{7,4},{8,11},{9,8},{10,9... | collective-permute-start | bytes 1572872 | tf_op jit(solution)/shard_map/ppermute | solution.py:54
  4.3 14.1 %collective-permute-start.1 = (bf16[256,1024]{1,0:T(8,128)(2,1)}, bf16[256,1024]{1,0:T(8,128)(2,1)}, u32[]{:S(2)}, u32[]{:S(2)}) collective-permute-start(bf16[256,1024]{1,0:T(8,128)(2,1)} %get-tuple-element.36.refs_0_), channel_id=1, source_target_pairs={{0,1},{1,2},{2,3},{3,0},{4,7},{5,4},{6,5},{7,6},{8,9},{9,10},{10,1... | collective-permute-start | bytes 1572872 | tf_op jit(solution)/shard_map/ppermute | solution.py:54
  5.5 2.4 %collective-permute-start = (s32[4,8]{1,0:T(4,128)S(1)}, s32[4,8]{1,0:T(4,128)S(1)}, u32[]{:S(2)}, u32[]{:S(2)}) collective-permute-start(s32[4,8]{1,0:T(4,128)S(1)} %copy-done.3), channel_id=1, source_target_pairs={{0,4},{4,0},{8,12},{12,8},{16,20},{20,16},{24,28},{28,24},{32,36},... | collective-permute-start | bytes 392 | tf_op jit(solution)/shard_map/ppermute | solution.py:50
  18.3 13.0 %collective-permute-start.3 = (bf16[256,1024]{1,0:T(8,128)(2,1)}, bf16[256,1024]{1,0:T(8,128)(2,1)S(1)}, u32[]{:S(2)}, u32[]{:S(2)}) collective-permute-start(bf16[256,1024]{1,0:T(8,128)(2,1)} %collective-permute-done.1.refs_1_), channel_id=1, source_target_pairs={{0,1},{1,2},{2,3},{3,0},{4,7},{5,4},{6,5},{7,6},{8,9},{9,10},{10,1... | collective-permute-start | bytes 1572872 | tf_op jit(solution)/shard_map/ppermute | solution.py:54
  19.8 27.4 %collective-permute-start.5 = (bf16[256,1024]{1,0:T(8,128)(2,1)S(1)}, bf16[256,1024]{1,0:T(8,128)(2,1)S(1)}, u32[]{:S(2)}, u32[]{:S(2)}) collective-permute-start(bf16[256,1024]{1,0:T(8,128)(2,1)S(1)} %get-tuple-element.27.refs_4_.refs_0_), channel_id=1, source_target_pairs={{0,3},{1,0},{2,1},{3,2},{4,5},{5,6},{6,7},{7,4},{8,11},{9,8},{10,9... | collective-permute-start | bytes 1572872 | tf_op jit(solution)/shard_map/ppermute | solution.py:54
  19.9 21.3 %collective-permute-start.4 = (bf16[256,1024]{1,0:T(8,128)(2,1)S(1)}, bf16[256,1024]{1,0:T(8,128)(2,1)S(1)}, u32[]{:S(2)}, u32[]{:S(2)}) collective-permute-start(bf16[256,1024]{1,0:T(8,128)(2,1)S(1)} %get-tuple-element.27.refs_4_.refs_0_), channel_id=1, source_target_pairs={{0,1},{1,2},{2,3},{3,0},{4,7},{5,4},{6,5},{7,6},{8,9},{9,10},{10,1... | collective-permute-start | bytes 1572872 | tf_op jit(solution)/shard_map/ppermute | solution.py:54
  22.5 1.6 copy-start.1
  32.4 4.3 %collective-permute-start.7 = (bf16[256,256]{1,0:T(8,128)(2,1)S(1)}, bf16[256,256]{1,0:T(8,128)(2,1)S(1)}, u32[]{:S(2)}, u32[]{:S(2)}) collective-permute-start(bf16[256,256]{1,0:T(8,128)(2,1)S(1)} %get-tuple-element.24), channel_id=1, source_target_pairs={{0,4},{4,0},{8,12},{12,8},{16,20},{20,16},{24,28},{28,24},{32,36},... | collective-permute-start | bytes 393224 | tf_op jit(solution)/shard_map/ppermute | solution.py:50
  36.7 7.1 %collective-permute-start.10 = (bf16[512,256]{1,0:T(8,128)(2,1)S(1)}, bf16[512,256]{1,0:T(8,128)(2,1)S(1)}, u32[]{:S(2)}, u32[]{:S(2)}) collective-permute-start(bf16[512,256]{1,0:T(8,128)(2,1)S(1)} %shard_map.76.refs_0_), channel_id=1, source_target_pairs={{0,64},{4,20},{8,72},{12,28},{16,80},{20,4},{24,88},{28,12},{32,96... | collective-permute-start | bytes 786440 | tf_op jit(solution)/shard_map/ppermute | solution.py:58
  39.7 7.3 %collective-permute-start.9 = (bf16[512,256]{1,0:T(8,128)(2,1)S(1)}, bf16[512,256]{1,0:T(8,128)(2,1)S(1)}, u32[]{:S(2)}, u32[]{:S(2)}) collective-permute-start(bf16[512,256]{1,0:T(8,128)(2,1)S(1)} %shard_map.76.refs_0_), channel_id=1, source_target_pairs={{0,96},{4,28},{8,104},{12,4},{16,112},{20,12},{24,120},{28,20},{32... | collective-permute-start | bytes 786440 | tf_op jit(solution)/shard_map/ppermute | solution.py:58
  40.4 6.7 %collective-permute-start.8 = (bf16[512,256]{1,0:T(8,128)(2,1)S(1)}, bf16[512,256]{1,0:T(8,128)(2,1)S(1)}, u32[]{:S(2)}, u32[]{:S(2)}) collective-permute-start(bf16[512,256]{1,0:T(8,128)(2,1)S(1)} %shard_map.76.refs_0_), channel_id=1, source_target_pairs={{0,32},{4,12},{8,40},{12,20},{16,48},{20,28},{24,56},{28,4},{32,64... | collective-permute-start | bytes 786440 | tf_op jit(solution)/shard_map/ppermute | solution.py:58
  41.1 8.3 %collective-permute-start.6 = (bf16[256,1024]{1,0:T(8,128)(2,1)S(1)}, bf16[256,1024]{1,0:T(8,128)(2,1)S(1)}, u32[]{:S(2)}, u32[]{:S(2)}) collective-permute-start(bf16[256,1024]{1,0:T(8,128)(2,1)S(1)} %collective-permute-done.4.refs_5_.refs_1_), channel_id=1, source_target_pairs={{0,1},{1,2},{2,3},{3,0},{4,7},{5,4},{6,5},{7,6},{8,9},{9,10},{10,1... | collective-permute-start | bytes 1572872 | tf_op jit(solution)/shard_map/ppermute | solution.py:54
  47.2 22.4 %slice-start = ((s8[8388608]{0:T(1024)(128)(4,1)}), s8[4194304]{0:T(1024)(128)(4,1)S(1)}, s32[]{:S(2)}) async-start(s8[8388608]{0:T(1024)(128)(4,1)} %bitcast.8), calls=%async_computation | async-start | bytes 8388608
  47.2 22.3 %slice-start.1 = ((s8[8388608]{0:T(1024)(128)(4,1)}), s8[4194304]{0:T(1024)(128)(4,1)S(1)}, s32[]{:S(2)}) async-start(s8[8388608]{0:T(1024)(128)(4,1)} %bitcast.8), calls=%async_computation.1 | async-start | bytes 8388608
  50.6 5.0 %collective-permute-start.14 = (bf16[256,256]{1,0:T(8,128)(2,1)S(1)}, bf16[256,256]{1,0:T(8,128)(2,1)S(1)}, u32[]{:S(2)}, u32[]{:S(2)}) collective-permute-start(bf16[256,256]{1,0:T(8,128)(2,1)S(1)} %get-tuple-element.31), channel_id=1, source_target_pairs={{0,4},{4,0},{8,12},{12,8},{16,20},{20,16},{24,28},{28,24},{32,36},... | collective-permute-start | bytes 393224 | tf_op jit(solution)/shard_map/ppermute | solution.py:50
  55.6 7.1 %collective-permute-start.17 = (bf16[512,256]{1,0:T(8,128)(2,1)S(1)}, bf16[512,256]{1,0:T(8,128)(2,1)S(1)}, u32[]{:S(2)}, u32[]{:S(2)}) collective-permute-start(bf16[512,256]{1,0:T(8,128)(2,1)S(1)} %shard_map.80.refs_0_), channel_id=1, source_target_pairs={{0,64},{4,20},{8,72},{12,28},{16,80},{20,4},{24,88},{28,12},{32,96... | collective-permute-start | bytes 786440 | tf_op jit(solution)/shard_map/ppermute | solution.py:58
  58.6 7.3 %collective-permute-start.16 = (bf16[512,256]{1,0:T(8,128)(2,1)S(1)}, bf16[512,256]{1,0:T(8,128)(2,1)S(1)}, u32[]{:S(2)}, u32[]{:S(2)}) collective-permute-start(bf16[512,256]{1,0:T(8,128)(2,1)S(1)} %shard_map.80.refs_0_), channel_id=1, source_target_pairs={{0,96},{4,28},{8,104},{12,4},{16,112},{20,12},{24,120},{28,20},{32... | collective-permute-start | bytes 786440 | tf_op jit(solution)/shard_map/ppermute | solution.py:58
  59.4 8.7 %collective-permute-start.15 = (bf16[512,256]{1,0:T(8,128)(2,1)S(1)}, bf16[512,256]{1,0:T(8,128)(2,1)S(1)}, u32[]{:S(2)}, u32[]{:S(2)}) collective-permute-start(bf16[512,256]{1,0:T(8,128)(2,1)S(1)} %shard_map.80.refs_0_), channel_id=1, source_target_pairs={{0,32},{4,12},{8,40},{12,20},{16,48},{20,28},{24,56},{28,4},{32,64... | collective-permute-start | bytes 786440 | tf_op jit(solution)/shard_map/ppermute | solution.py:58
  60.1 20.2 %collective-permute-start.11 = (bf16[2048,256]{1,0:T(8,128)(2,1)S(1)}, bf16[2048,256]{1,0:T(8,128)(2,1)S(1)}, u32[]{:S(2)}, u32[]{:S(2)}) collective-permute-start(bf16[2048,256]{1,0:T(8,128)(2,1)S(1)} %shard_map.77.rest_0_), channel_id=1, source_target_pairs={{0,8},{4,36},{8,16},{12,44},{16,24},{20,52},{24,0},{28,60},{32,40}... | collective-permute-start | bytes 3145736 | tf_op jit(solution)/shard_map/ppermute | solution.py:62
  68.2 14.0 %collective-permute-start.19 = (bf16[2048,256]{1,0:T(8,128)(2,1)S(1)}, bf16[2048,256]{1,0:T(8,128)(2,1)S(1)}, u32[]{:S(2)}, u32[]{:S(2)}) collective-permute-start(bf16[2048,256]{1,0:T(8,128)(2,1)S(1)} %shard_map.81.rest_4_), channel_id=1, source_target_pairs={{0,24},{4,100},{8,0},{12,108},{16,8},{20,116},{24,16},{28,124},{32... | collective-permute-start | bytes 3145736 | tf_op jit(solution)/shard_map/ppermute | solution.py:62
  68.5 24.9 %collective-permute-start.12 = (bf16[2048,256]{1,0:T(8,128)(2,1)S(1)}, bf16[2048,256]{1,0:T(8,128)(2,1)S(1)}, u32[]{:S(2)}, u32[]{:S(2)}) collective-permute-start(bf16[2048,256]{1,0:T(8,128)(2,1)S(1)} %shard_map.77.rest_0_), channel_id=1, source_target_pairs={{0,24},{4,100},{8,0},{12,108},{16,8},{20,116},{24,16},{28,124},{32... | collective-permute-start | bytes 3145736 | tf_op jit(solution)/shard_map/ppermute | solution.py:62
  74.7 31.6 %copy-start.2 = (s32[16]{0:T(128)S(1)}, s32[16]{0:T(128)}, u32[]{:S(2)}) copy-start(s32[16]{0:T(128)} %lengths.11) | copy-start | bytes 196
  79.8 15.2 %collective-permute-start.18 = (bf16[2048,256]{1,0:T(8,128)(2,1)S(1)}, bf16[2048,256]{1,0:T(8,128)(2,1)S(1)}, u32[]{:S(2)}, u32[]{:S(2)}) collective-permute-start(bf16[2048,256]{1,0:T(8,128)(2,1)S(1)} %shard_map.81.rest_4_), channel_id=1, source_target_pairs={{0,8},{4,36},{8,16},{12,44},{16,24},{20,52},{24,0},{28,60},{32,40}... | collective-permute-start | bytes 3145736 | tf_op jit(solution)/shard_map/ppermute | solution.py:62
  80.3 26.0 %collective-permute-start.13 = (bf16[2048,256]{1,0:T(8,128)(2,1)S(1)}, bf16[2048,256]{1,0:T(8,128)(2,1)S(1)}, u32[]{:S(2)}, u32[]{:S(2)}) collective-permute-start(bf16[2048,256]{1,0:T(8,128)(2,1)S(1)} %collective-permute-done.11.rest_1_), channel_id=1, source_target_pairs={{0,8},{4,36},{8,16},{12,44},{16,24},{20,52},{24,0},{28,60},{32,40}... | collective-permute-start | bytes 3145736 | tf_op jit(solution)/shard_map/ppermute | solution.py:62
  82.2 24.0 %collective-permute-start.20 = (bf16[2048,256]{1,0:T(8,128)(2,1)S(1)}, bf16[2048,256]{1,0:T(8,128)(2,1)S(1)}, u32[]{:S(2)}, u32[]{:S(2)}) collective-permute-start(bf16[2048,256]{1,0:T(8,128)(2,1)S(1)} %collective-permute-done.19.rest_6_), channel_id=1, source_target_pairs={{0,24},{4,100},{8,0},{12,108},{16,8},{20,116},{24,16},{28,124},{32... | collective-permute-start | bytes 3145736 | tf_op jit(solution)/shard_map/ppermute | solution.py:62
  83.4 7.5 %collective-permute-start.21 = (bf16[512,512]{1,0:T(8,128)(2,1)S(1)}, bf16[512,512]{1,0:T(8,128)(2,1)S(1)}, u32[]{:S(2)}, u32[]{:S(2)}) collective-permute-start(bf16[512,512]{1,0:T(8,128)(2,1)S(1)} %shard_map.82), channel_id=1, source_target_pairs={{0,4},{4,0},{8,12},{12,8},{16,20},{20,16},{24,28},{28,24},{32,36},... | collective-permute-start | bytes 1572872 | tf_op jit(solution)/shard_map/ppermute | solution.py:50
  106.2 10.8 %slice-start.2 = ((s8[8388608]{0:T(1024)(128)(4,1)}), s8[4194304]{0:T(1024)(128)(4,1)S(1)}, s32[]{:S(2)}) async-start(s8[8388608]{0:T(1024)(128)(4,1)} %bitcast.10), calls=%async_computation.2 | async-start | bytes 8388608
  108.6 8.5 %slice-start.3 = ((s8[8388608]{0:T(1024)(128)(4,1)}), s8[4194304]{0:T(1024)(128)(4,1)S(1)}, s32[]{:S(2)}) async-start(s8[8388608]{0:T(1024)(128)(4,1)} %bitcast.10), calls=%async_computation.3 | async-start | bytes 8388608
  108.6 8.5 %collective-permute-start.24 = (bf16[128,512]{1,0:T(8,128)(2,1)S(1)}, bf16[128,512]{1,0:T(8,128)(2,1)S(1)}, u32[]{:S(2)}, u32[]{:S(2)}) collective-permute-start(bf16[128,512]{1,0:T(8,128)(2,1)S(1)} %shard_map.90), channel_id=1, source_target_pairs={{0,4},{4,0},{8,12},{12,8},{16,20},{20,16},{24,28},{28,24},{32,36},... | collective-permute-start | bytes 393224 | tf_op jit(solution)/shard_map/ppermute | solution.py:50
  120.4 14.0 %collective-permute-start.25 = (bf16[128,4096]{1,0:T(8,128)(2,1)S(1)}, bf16[128,4096]{1,0:T(8,128)(2,1)S(1)}, u32[]{:S(2)}, u32[]{:S(2)}) collective-permute-start(bf16[128,4096]{1,0:T(8,128)(2,1)S(1)} %shard_map.91), channel_id=1, source_target_pairs={{0,1},{1,2},{2,3},{3,0},{4,7},{5,4},{6,5},{7,6},{8,9},{9,10},{10,1... | collective-permute-start | bytes 3145736 | tf_op jit(solution)/shard_map/ppermute | solution.py:54
  124.0 3.6 %collective-permute-start.23 = (bf16[256,512]{1,0:T(8,128)(2,1)S(1)}, bf16[256,512]{1,0:T(8,128)(2,1)S(1)}, u32[]{:S(2)}, u32[]{:S(2)}) collective-permute-start(bf16[256,512]{1,0:T(8,128)(2,1)S(1)} %shard_map.87), channel_id=1, source_target_pairs={{0,4},{4,0},{8,12},{12,8},{16,20},{20,16},{24,28},{28,24},{32,36},... | collective-permute-start | bytes 786440 | tf_op jit(solution)/shard_map/ppermute | solution.py:50
  132.1 21.7 %collective-permute-start.27 = (bf16[128,4096]{1,0:T(8,128)(2,1)S(1)}, bf16[128,4096]{1,0:T(8,128)(2,1)S(1)}, u32[]{:S(2)}, u32[]{:S(2)}) collective-permute-start(bf16[128,4096]{1,0:T(8,128)(2,1)S(1)} %get-tuple-element.34), channel_id=1, source_target_pairs={{0,3},{1,0},{2,1},{3,2},{4,5},{5,6},{6,7},{7,4},{8,11},{9,8},{10,9... | collective-permute-start | bytes 3145736 | tf_op jit(solution)/shard_map/ppermute | solution.py:54
  134.7 23.6 %collective-permute-start.26 = (bf16[128,4096]{1,0:T(8,128)(2,1)S(1)}, bf16[128,4096]{1,0:T(8,128)(2,1)S(1)}, u32[]{:S(2)}, u32[]{:S(2)}) collective-permute-start(bf16[128,4096]{1,0:T(8,128)(2,1)S(1)} %add_convert_fusion.1), channel_id=1, source_target_pairs={{0,1},{1,2},{2,3},{3,0},{4,7},{5,4},{6,5},{7,6},{8,9},{9,10},{10,1... | collective-permute-start | bytes 3145736 | tf_op jit(solution)/shard_map/ppermute | solution.py:54
  138.0 3.6 %collective-permute-start.22 = (bf16[128,512]{1,0:T(8,128)(2,1)S(1)}, bf16[128,512]{1,0:T(8,128)(2,1)S(1)}, u32[]{:S(2)}, u32[]{:S(2)}) collective-permute-start(bf16[128,512]{1,0:T(8,128)(2,1)S(1)} %shard_map.84), channel_id=1, source_target_pairs={{0,4},{4,0},{8,12},{12,8},{16,20},{20,16},{24,28},{28,24},{32,36},... | collective-permute-start | bytes 393224 | tf_op jit(solution)/shard_map/ppermute | solution.py:50

commit v2 on v1

--- a/solution.py
+++ b/solution.py
@@ -364,17 +364,19 @@
         gathered += [line, near[1], near[-1], send_two(onward, way)]
     query[1] = core_swap(query[1])
 
-    def attended(*steps):
-        other = core_swap(attend(1, steps, ids, table, doc_lengths, query[1], gathered))
-        return attend(0, steps, ids, table, doc_lengths, query[0], gathered), other
+    def attended(step, *earlier):
+        known = after(ids, *earlier)
+        other = core_swap(attend(1, (step,), known, table, doc_lengths, query[1], gathered))
+        return attend(0, (step,), known, table, doc_lengths, query[0], gathered), other
 
     core_id = ids[4:5]
     (far,) = project_out(core_id, *attended(2), w_output, (BF16,))
     arrived = send_tp(far, 1)
-    ahead, behind = project_out(core_id, *attended(1, -1), w_output, (F32, BF16))
+    (behind,) = project_out(core_id, *attended(-1, far), w_output, (BF16,))
     from_after = send_tp(behind, -1)
+    (ahead,) = project_out(core_id, *attended(1, behind), w_output, (F32,))
     from_before = send_tp((ahead + arrived.astype(F32)).astype(BF16), 1)
-    (own,) = project_out(core_id, *attended(0), w_output, (F32,))
+    (own,) = project_out(core_id, *attended(0, ahead), w_output, (F32,))
     return (own + from_before.astype(F32) + from_after.astype(F32)).astype(BF16)
 
 

time: 160 us -> 158 us (0.988)
  waiting for transfers between devices: 60.9 us -> 49.1 us
  starting transfers between devices: 45.9 us -> 51.1 us
  Pallas kernels: 45.2 us -> 49.6 us
    ppermute x9, waiting for transfers between devices: 28.4 us -> 17.4 us  [send_tp(): return lax.ppermute(u, ('ctx', 'tp'), tp_pairs(step))]
    ppermute x7 -> x8, starting transfers between devices: 21.7 us -> 26.5 us  [core_swap(): return lax.ppermute(u, 'ctx', CORE_PAIRS)]
    pallas_call x3 -> x4, Pallas kernels: 11.2 us -> 13.4 us  [project_out(): pl.pallas_call(out_kernel, grid_spec=pltpu.PrefetchScalarGridSpec(num_sca...]
    pallas_call x6 -> x8, Pallas kernels: 16.2 us -> 18.4 us  [attend(): pl.pallas_call(functools.partial(attend_kernel, side, steps, len(arrays))...]
    ppermute x7 -> x8, waiting for transfers between devices: 3.52 us -> 3.52 us  [core_swap(): return lax.ppermute(u, 'ctx', CORE_PAIRS)]
  transfers between devices with their start and end apart: 28 -> 29, of which waited for: 19 -> 17; matrix products, arithmetic and copies ran while one was open for 1% -> 1% of each run, Pallas kernels for 24% -> 27%
where the time goes in v2:
time: 158 us; the launch traced here: 157 us
  starting transfers between devices  51.1 us (32%)
  Pallas kernels  49.6 us (31%)
  waiting for transfers between devices  49.1 us (31%)
  local copies, waits for them, and re-layouts  4.01 us (3%)
  other arithmetic  3.19 us (2%)
    ppermute x8, starting transfers between devices, core_swap(): return lax.ppermute(u, 'ctx', CORE_PAIRS)  26.5 us
    pallas_call x8, Pallas kernels, attend(): pl.pallas_call(functools.partial(attend_kernel, side, steps, len(arrays))...  18.4 us
    ppermute x9, waiting for transfers between devices, send_tp(): return lax.ppermute(u, ('ctx', 'tp'), tp_pairs(step))  17.4 us
    ppermute x6, waiting for transfers between devices, send_two(): return lax.ppermute(u, 'ctx', plane_pairs(step, False))  15.2 us
    pallas_call x4, Pallas kernels, project_out(): pl.pallas_call(out_kernel, grid_spec=pltpu.PrefetchScalarGridSpec(num_sca...  13.4 us
    ppermute x6, waiting for transfers between devices, send_one(): return lax.ppermute(u, 'ctx', plane_pairs(step, True))  13 us
    pallas_call x2, Pallas kernels, project_q(): pl.pallas_call(q_kernel, grid_spec=pltpu.PrefetchScalarGridSpec(num_scala...  10.2 us
    ppermute x9, starting transfers between devices, send_tp(): return lax.ppermute(u, ('ctx', 'tp'), tp_pairs(step))  9.89 us
  transfers between devices with their start and end apart: 29, of which 17 were waited for; matrix products, arithmetic and copies ran while one was open for 1% of the time, Pallas kernels for 27%

profile of v2, /device:TPU:1, one launch (start us, length us, event | category | flops | bytes accessed | tf_op | source)
XLA Modules:
  0.0 157.4 jit_solution(13045120706897720026)
XLA Ops:
  0.0 2.2 %fusion.27 = (bf16[256,1024]{1,0:T(8,128)(2,1)S(1)}, bf16[256,1024]{1,0:T(8,128)(2,1)}) fusion(bf16[512,1024]{1,0:T(8,128)(2,1)} %param.7), kind=kLoop, calls=%fused_computation.73 | loop fusion | bytes 2097152 | tf_op jit(solution)/shard_map/slice | solution.py:338
  2.2 3.3 %collective-permute-start.1 = (bf16[256,1024]{1,0:T(8,128)(2,1)}, bf16[256,1024]{1,0:T(8,128)(2,1)}, u32[]{:S(2)}, u32[]{:S(2)}) collective-permute-start(bf16[256,1024]{1,0:T(8,128)(2,1)} %get-tuple-element.38.refs_0_), channel_id=1, source_target_pairs={{0,1},{1,2},{2,3},{3,0},{4,7},{5,4},{6,5},{7,6},{8,9},{9,10},{10,1... | collective-permute-start | bytes 1572872 | tf_op jit(solution)/shard_map/ppermute | solution.py:54
  5.5 1.3 collective-permute-start
  7.0 1.0 fusion
  8.3 0.3 and_reduce_fusion
  8.7 7.3 %collective-permute-done.1.refs_1_ = bf16[256,1024]{1,0:T(8,128)(2,1)} collective-permute-done((bf16[256,1024]{1,0:T(8,128)(2,1)}, bf16[256,1024]{1,0:T(8,128)(2,1)}, u32[]{:S(2)}, u32[]{:S(2)}) %collective-permute-start.1) | collective-permute-done | bytes 524320 | tf_op jit(solution)/shard_map/ppermute | solution.py:54
  16.0 3.4 %collective-permute-start.3 = (bf16[256,1024]{1,0:T(8,128)(2,1)}, bf16[256,1024]{1,0:T(8,128)(2,1)S(1)}, u32[]{:S(2)}, u32[]{:S(2)}) collective-permute-start(bf16[256,1024]{1,0:T(8,128)(2,1)} %collective-permute-done.1.refs_1_), channel_id=1, source_target_pairs={{0,1},{1,2},{2,3},{3,0},{4,7},{5,4},{6,5},{7,6},{8,9},{9,10},{10,1... | collective-permute-start | bytes 1572872 | tf_op jit(solution)/shard_map/ppermute | solution.py:54
  19.4 0.4 collective-permute-start.4
  19.8 1.1 collective-permute-start.5
  20.9 1.6 %copy-done.1 = bf16[4096,256]{1,0:T(8,128)(2,1)S(1)} copy-done((bf16[4096,256]{1,0:T(8,128)(2,1)S(1)}, bf16[4096,256]{1,0:T(8,128)(2,1)}, u32[]{:S(2)}) %copy-start.1) | copy-done | bytes 2097176
  22.5 3.3 %shard_map.73 = (f32[256,256]{1,0:T(8,128)S(1)}, f32[256,256]{1,0:T(8,128)S(1)}) custom-call(s32[8]{0:T(128)S(1)} %stack.35.ids, bf16[256,1024]{1,0:T(8,128)(2,1)} %get-tuple-element.38.refs_0_, bf16[256,1024]{1,0:T(8,128)(2,1)} %collective-permute-done.1.refs_1_, bf16[256,1024]{1,0:T(8,128)(2,1)} %collective-permute-done.2.refs_2_, ...), custom_call_target="tpu_custom_call" | custom-call | flops 3300000000 | tf_op jit(solution)/shard_map/pallas_call | solution.py:90
  25.8 1.6 %collective-permute-done.3.far.refs_3_ = bf16[256,1024]{1,0:T(8,128)(2,1)S(1)} collective-permute-done((bf16[256,1024]{1,0:T(8,128)(2,1)}, bf16[256,1024]{1,0:T(8,128)(2,1)S(1)}, u32[]{:S(2)}, u32[]{:S(2)}) %collective-permute-start.3) | collective-permute-done | bytes 524320 | tf_op jit(solution)/shard_map/ppermute | solution.py:54
  27.4 1.1 shard_map.74
  28.5 6.8 %collective-permute-start.7 = (bf16[256,256]{1,0:T(8,128)(2,1)S(1)}, bf16[256,256]{1,0:T(8,128)(2,1)S(1)}, u32[]{:S(2)}, u32[]{:S(2)}) collective-permute-start(bf16[256,256]{1,0:T(8,128)(2,1)S(1)} %get-tuple-element.25), channel_id=1, source_target_pairs={{0,4},{4,0},{8,12},{12,8},{16,20},{20,16},{24,28},{28,24},{32,36},... | collective-permute-start | bytes 393224 | tf_op jit(solution)/shard_map/ppermute | solution.py:50
  35.3 1.0 collective-permute-done.7.refs_1_
  36.3 1.8 %collective-permute-start.8 = (bf16[512,256]{1,0:T(8,128)(2,1)S(1)}, bf16[512,256]{1,0:T(8,128)(2,1)S(1)}, u32[]{:S(2)}, u32[]{:S(2)}) collective-permute-start(bf16[512,256]{1,0:T(8,128)(2,1)S(1)} %shard_map.76.refs_0_), channel_id=1, source_target_pairs={{0,32},{4,12},{8,40},{12,20},{16,48},{20,28},{24,56},{28,4},{32,64... | collective-permute-start | bytes 786440 | tf_op jit(solution)/shard_map/ppermute | solution.py:58
  38.1 1.5 collective-permute-start.9
  39.6 1.6 collective-permute-start.10
  41.1 2.4 %collective-permute-done.8.refs_1_ = bf16[512,256]{1,0:T(8,128)(2,1)S(1)} collective-permute-done((bf16[512,256]{1,0:T(8,128)(2,1)S(1)}, bf16[512,256]{1,0:T(8,128)(2,1)S(1)}, u32[]{:S(2)}, u32[]{:S(2)}) %collective-permute-start.8) | collective-permute-done | bytes 262176 | tf_op jit(solution)/shard_map/ppermute | solution.py:58
  43.6 2.2 %collective-permute-done.9.refs_2_ = bf16[512,256]{1,0:T(8,128)(2,1)S(1)} collective-permute-done((bf16[512,256]{1,0:T(8,128)(2,1)S(1)}, bf16[512,256]{1,0:T(8,128)(2,1)S(1)}, u32[]{:S(2)}, u32[]{:S(2)}) %collective-permute-start.9) | collective-permute-done | bytes 262176 | tf_op jit(solution)/shard_map/ppermute | solution.py:58
  45.7 1.8 %collective-permute-done.10.refs_3_ = bf16[512,256]{1,0:T(8,128)(2,1)S(1)} collective-permute-done((bf16[512,256]{1,0:T(8,128)(2,1)S(1)}, bf16[512,256]{1,0:T(8,128)(2,1)S(1)}, u32[]{:S(2)}, u32[]{:S(2)}) %collective-permute-start.10) | collective-permute-done | bytes 262176 | tf_op jit(solution)/shard_map/ppermute | solution.py:58
  47.6 2.0 %shard_map.78 = (f32[256,256]{1,0:T(8,128)S(1)}, f32[256,256]{1,0:T(8,128)S(1)}) custom-call(s32[8]{0:T(128)S(1)} %stack.35.ids, bf16[256,1024]{1,0:T(8,128)(2,1)S(1)} %get-tuple-element.28.refs_4_.refs_0_, bf16[256,1024]{1,0:T(8,128)(2,1)S(1)} %collective-permute-done.4.refs_5_.refs_1_, bf16[256,1024]{1,0:T(8,128)(2,1)S(1)} %collective-permute-done.5.refs_6_.refs_2_, ...), custom_call_target="tpu_custom_call" | custom-call | flops 3300000000 | tf_op jit(solution)/shard_map/pallas_call | solution.py:90
  49.6 1.1 shard_map.79
  50.7 3.9 %collective-permute-start.14 = (bf16[256,256]{1,0:T(8,128)(2,1)S(1)}, bf16[256,256]{1,0:T(8,128)(2,1)S(1)}, u32[]{:S(2)}, u32[]{:S(2)}) collective-permute-start(bf16[256,256]{1,0:T(8,128)(2,1)S(1)} %get-tuple-element.32), channel_id=1, source_target_pairs={{0,4},{4,0},{8,12},{12,8},{16,20},{20,16},{24,28},{28,24},{32,36},... | collective-permute-start | bytes 393224 | tf_op jit(solution)/shard_map/ppermute | solution.py:50
  54.6 1.0 collective-permute-done.14.refs_1_
  55.6 1.4 collective-permute-start.15
  57.0 1.5 collective-permute-start.16
  58.5 1.6 collective-permute-start.17
  60.1 0.7 collective-permute-start.11
  60.8 1.7 %collective-permute-done.15.refs_1_ = bf16[512,256]{1,0:T(8,128)(2,1)S(1)} collective-permute-done((bf16[512,256]{1,0:T(8,128)(2,1)S(1)}, bf16[512,256]{1,0:T(8,128)(2,1)S(1)}, u32[]{:S(2)}, u32[]{:S(2)}) %collective-permute-start.15) | collective-permute-done | bytes 262176 | tf_op jit(solution)/shard_map/ppermute | solution.py:58
  62.5 2.2 %collective-permute-done.16.refs_2_ = bf16[512,256]{1,0:T(8,128)(2,1)S(1)} collective-permute-done((bf16[512,256]{1,0:T(8,128)(2,1)S(1)}, bf16[512,256]{1,0:T(8,128)(2,1)S(1)}, u32[]{:S(2)}, u32[]{:S(2)}) %collective-permute-start.16) | collective-permute-done | bytes 262176 | tf_op jit(solution)/shard_map/ppermute | solution.py:58
  64.6 2.8 %collective-permute-done.17.refs_3_ = bf16[512,256]{1,0:T(8,128)(2,1)S(1)} collective-permute-done((bf16[512,256]{1,0:T(8,128)(2,1)S(1)}, bf16[512,256]{1,0:T(8,128)(2,1)S(1)}, u32[]{:S(2)}, u32[]{:S(2)}) %collective-permute-start.17) | collective-permute-done | bytes 262176 | tf_op jit(solution)/shard_map/ppermute | solution.py:58
  67.5 0.9 collective-permute-start.19
  68.3 0.3 collective-permute-start.12
  68.6 5.1 %shard_map.75.query = bf16[512,512]{1,0:T(8,128)(2,1)S(1)} custom-call(s32[8]{0:T(128)S(1)} %stack.35.ids, bf16[256,1024]{1,0:T(8,128)(2,1)} %get-tuple-element.38.refs_0_, bf16[256,1024]{1,0:T(8,128)(2,1)} %collective-permute-done.1.refs_1_, bf16[256,1024]{1,0:T(8,128)(2,1)} %collective-permute-done.2.refs_2_, ...), custom_call_target="tpu_custom_call" | custom-call | flops 5500000256 | tf_op jit(solution)/shard_map/pallas_call | solution.py:159
  73.7 5.1 %shard_map.82 = bf16[512,512]{1,0:T(8,128)(2,1)S(1)} custom-call(s32[8]{0:T(128)S(1)} %stack.35.ids, bf16[256,1024]{1,0:T(8,128)(2,1)} %get-tuple-element.38.refs_0_, bf16[256,1024]{1,0:T(8,128)(2,1)} %collective-permute-done.1.refs_1_, bf16[256,1024]{1,0:T(8,128)(2,1)} %collective-permute-done.2.refs_2_, ...), custom_call_target="tpu_custom_call" | custom-call | flops 5500000256 | tf_op jit(solution)/shard_map/pallas_call | solution.py:159
  78.8 1.3 collective-permute-start.18
  80.1 0.7 collective-permute-start.13
  80.8 0.7 collective-permute-done.19.rest_6_
  81.5 1.7 %collective-permute-start.20 = (bf16[2048,256]{1,0:T(8,128)(2,1)S(1)}, bf16[2048,256]{1,0:T(8,128)(2,1)S(1)}, u32[]{:S(2)}, u32[]{:S(2)}) collective-permute-start(bf16[2048,256]{1,0:T(8,128)(2,1)S(1)} %collective-permute-done.19.rest_6_), channel_id=1, source_target_pairs={{0,24},{4,100},{8,0},{12,108},{16,8},{20,116},{24,16},{28,124},{32... | collective-permute-start | bytes 3145736 | tf_op jit(solution)/shard_map/ppermute | solution.py:62
  83.2 6.1 %collective-permute-start.21 = (bf16[512,512]{1,0:T(8,128)(2,1)S(1)}, bf16[512,512]{1,0:T(8,128)(2,1)S(1)}, u32[]{:S(2)}, u32[]{:S(2)}) collective-permute-start(bf16[512,512]{1,0:T(8,128)(2,1)S(1)} %shard_map.82), channel_id=1, source_target_pairs={{0,4},{4,0},{8,12},{12,8},{16,20},{20,16},{24,28},{28,24},{32,36},... | collective-permute-start | bytes 1572872 | tf_op jit(solution)/shard_map/ppermute | solution.py:50
  89.3 1.5 collective-permute-done.21.query
  90.8 1.9 %collective-permute-done.12.rest_2_ = bf16[2048,256]{1,0:T(8,128)(2,1)S(1)} collective-permute-done((bf16[2048,256]{1,0:T(8,128)(2,1)S(1)}, bf16[2048,256]{1,0:T(8,128)(2,1)S(1)}, u32[]{:S(2)}, u32[]{:S(2)}) %collective-permute-start.12) | collective-permute-done | bytes 1048608 | tf_op jit(solution)/shard_map/ppermute | solution.py:62
  92.7 1.3 collective-permute-done.18.rest_5_
  94.0 11.2 %collective-permute-done.13.rest_3_ = bf16[2048,256]{1,0:T(8,128)(2,1)S(1)} collective-permute-done((bf16[2048,256]{1,0:T(8,128)(2,1)S(1)}, bf16[2048,256]{1,0:T(8,128)(2,1)S(1)}, u32[]{:S(2)}, u32[]{:S(2)}) %collective-permute-start.13) | collective-permute-done | bytes 1048608 | tf_op jit(solution)/shard_map/ppermute | solution.py:62
  105.3 2.3 %shard_map.84 = bf16[128,512]{1,0:T(8,128)(2,1)S(1)} custom-call(s32[8]{0:T(128)S(1)} %stack.35.ids, s32[128]{0:T(128)S(1)} %reshape.29.table, s32[16]{0:T(128)S(1)} %copy-done.2, bf16[512,512]{1,0:T(8,128)(2,1)S(1)} %collective-permute-done.21.query, bf16[2048,256]{1,0:T(8,128)(2,1)S(1)} %shard_map.77.rest_0_, ...), custom_call_target="tpu_custom_call" | custom-call | flops 2420000000 | tf_op jit(solution)/shard_map/pallas_call | solution.py:251
  107.6 6.3 %collective-permute-start.22 = (bf16[128,512]{1,0:T(8,128)(2,1)S(1)}, bf16[128,512]{1,0:T(8,128)(2,1)S(1)}, u32[]{:S(2)}, u32[]{:S(2)}) collective-permute-start(bf16[128,512]{1,0:T(8,128)(2,1)S(1)} %shard_map.84), channel_id=1, source_target_pairs={{0,4},{4,0},{8,12},{12,8},{16,20},{20,16},{24,28},{28,24},{32,36},... | collective-permute-start | bytes 393224 | tf_op jit(solution)/shard_map/ppermute | solution.py:50
  113.9 2.3 %shard_map.83.mine = bf16[128,512]{1,0:T(8,128)(2,1)S(1)} custom-call(s32[8]{0:T(128)S(1)} %stack.35.ids, s32[128]{0:T(128)S(1)} %reshape.29.table, s32[16]{0:T(128)S(1)} %copy-done.2, bf16[512,512]{1,0:T(8,128)(2,1)S(1)} %shard_map.75.query, bf16[2048,256]{1,0:T(8,128)(2,1)S(1)} %shard_map.77.rest_0_, ...), custom_call_target="tpu_custom_call" | custom-call | flops 2420000000 | tf_op jit(solution)/shard_map/pallas_call | solution.py:251
  116.2 3.3 %shard_map.85 = bf16[128,4096]{1,0:T(8,128)(2,1)S(1)} custom-call(s32[1]{0:T(128)} %bitcast.core, bf16[128,512]{1,0:T(8,128)(2,1)S(1)} %shard_map.83.mine, bf16[128,512]{1,0:T(8,128)(2,1)S(1)} %collective-permute-done.22.other, bf16[1024,4096]{1,0:T(8,128)(2,1)S(1)} %bitcast.11), custom_call_target="tpu_custom_call" | custom-call | flops 3300000000 | tf_op jit(solution)/shard_map/pallas_call | solution.py:281
  119.6 2.3 %shard_map.87 = bf16[128,512]{1,0:T(8,128)(2,1)S(1)} custom-call(s32[8]{0:T(128)S(1)} %stack.35.ids, s32[128]{0:T(128)S(1)} %reshape.29.table, s32[16]{0:T(128)S(1)} %copy-done.2, bf16[512,512]{1,0:T(8,128)(2,1)S(1)} %collective-permute-done.21.query, bf16[2048,256]{1,0:T(8,128)(2,1)S(1)} %shard_map.77.rest_0_, ...), custom_call_target="tpu_custom_call" | custom-call | flops 2420000000 | tf_op jit(solution)/shard_map/pallas_call | solution.py:251
  122.0 2.5 %shard_map.86.mine = bf16[128,512]{1,0:T(8,128)(2,1)S(1)} custom-call(s32[8]{0:T(128)S(1)} %stack.35.ids, s32[128]{0:T(128)S(1)} %reshape.29.table, s32[16]{0:T(128)S(1)} %copy-done.2, bf16[512,512]{1,0:T(8,128)(2,1)S(1)} %shard_map.75.query, bf16[2048,256]{1,0:T(8,128)(2,1)S(1)} %shard_map.77.rest_0_, ...), custom_call_target="tpu_custom_call" | custom-call | flops 2420000000 | tf_op jit(solution)/shard_map/pallas_call | solution.py:251
  124.5 3.3 %shard_map.88 = bf16[128,4096]{1,0:T(8,128)(2,1)S(1)} custom-call(s32[1]{0:T(128)} %bitcast.core, bf16[128,512]{1,0:T(8,128)(2,1)S(1)} %shard_map.86.mine, bf16[128,512]{1,0:T(8,128)(2,1)S(1)} %collective-permute-done.23.other, bf16[1024,4096]{1,0:T(8,128)(2,1)S(1)} %bitcast.11), custom_call_target="tpu_custom_call" | custom-call | flops 3300000000 | tf_op jit(solution)/shard_map/pallas_call | solution.py:281
  127.8 1.5 collective-permute-start.28
  129.3 2.2 %shard_map.90 = bf16[128,512]{1,0:T(8,128)(2,1)S(1)} custom-call(s32[8]{0:T(128)S(1)} %stack.35.ids, s32[128]{0:T(128)S(1)} %reshape.29.table, s32[16]{0:T(128)S(1)} %copy-done.2, bf16[512,512]{1,0:T(8,128)(2,1)S(1)} %collective-permute-done.21.query, bf16[2048,256]{1,0:T(8,128)(2,1)S(1)} %shard_map.77.rest_0_, ...), custom_call_target="tpu_custom_call" | custom-call | flops 2420000000 | tf_op jit(solution)/shard_map/pallas_call | solution.py:251
  131.6 1.9 %collective-permute-start.24 = (bf16[128,512]{1,0:T(8,128)(2,1)S(1)}, bf16[128,512]{1,0:T(8,128)(2,1)S(1)}, u32[]{:S(2)}, u32[]{:S(2)}) collective-permute-start(bf16[128,512]{1,0:T(8,128)(2,1)S(1)} %shard_map.90), channel_id=1, source_target_pairs={{0,4},{4,0},{8,12},{12,8},{16,20},{20,16},{24,28},{28,24},{32,36},... | collective-permute-start | bytes 393224 | tf_op jit(solution)/shard_map/ppermute | solution.py:50
  133.5 2.3 %shard_map.89.mine = bf16[128,512]{1,0:T(8,128)(2,1)S(1)} custom-call(s32[8]{0:T(128)S(1)} %stack.35.ids, s32[128]{0:T(128)S(1)} %reshape.29.table, s32[16]{0:T(128)S(1)} %copy-done.2, bf16[512,512]{1,0:T(8,128)(2,1)S(1)} %shard_map.75.query, bf16[2048,256]{1,0:T(8,128)(2,1)S(1)} %shard_map.77.rest_0_, ...), custom_call_target="tpu_custom_call" | custom-call | flops 2420000000 | tf_op jit(solution)/shard_map/pallas_call | solution.py:251
  135.8 3.4 %shard_map.91 = f32[128,4096]{1,0:T(8,128)S(1)} custom-call(s32[1]{0:T(128)} %bitcast.core, bf16[128,512]{1,0:T(8,128)(2,1)S(1)} %shard_map.89.mine, bf16[128,512]{1,0:T(8,128)(2,1)S(1)} %collective-permute-done.24.other, bf16[1024,4096]{1,0:T(8,128)(2,1)S(1)} %bitcast.11), custom_call_target="tpu_custom_call" | custom-call | flops 3300000000 | tf_op jit(solution)/shard_map/pallas_call | solution.py:281
  139.2 0.2 add_convert_fusion.1
  139.5 2.2 %shard_map.93 = bf16[128,512]{1,0:T(8,128)(2,1)S(1)} custom-call(s32[8]{0:T(128)S(1)} %stack.35.ids, s32[128]{0:T(128)S(1)} %reshape.29.table, s32[16]{0:T(128)S(1)} %copy-done.2, bf16[512,512]{1,0:T(8,128)(2,1)S(1)} %collective-permute-done.21.query, bf16[2048,256]{1,0:T(8,128)(2,1)S(1)} %shard_map.77.rest_0_, ...), custom_call_target="tpu_custom_call" | custom-call | flops 2420000000 | tf_op jit(solution)/shard_map/pallas_call | solution.py:251
  141.9 2.2 %shard_map.92.mine = bf16[128,512]{1,0:T(8,128)(2,1)S(1)} custom-call(s32[8]{0:T(128)S(1)} %stack.35.ids, s32[128]{0:T(128)S(1)} %reshape.29.table, s32[16]{0:T(128)S(1)} %copy-done.2, bf16[512,512]{1,0:T(8,128)(2,1)S(1)} %shard_map.75.query, bf16[2048,256]{1,0:T(8,128)(2,1)S(1)} %shard_map.77.rest_0_, ...), custom_call_target="tpu_custom_call" | custom-call | flops 2420000000 | tf_op jit(solution)/shard_map/pallas_call | solution.py:251
  144.1 3.4 %shard_map.94 = f32[128,4096]{1,0:T(8,128)S(1)} custom-call(s32[1]{0:T(128)} %bitcast.core, bf16[128,512]{1,0:T(8,128)(2,1)S(1)} %shard_map.92.mine, bf16[128,512]{1,0:T(8,128)(2,1)S(1)} %collective-permute-done.25.other, bf16[1024,4096]{1,0:T(8,128)(2,1)S(1)} %bitcast.11), custom_call_target="tpu_custom_call" | custom-call | flops 3300000000 | tf_op jit(solution)/shard_map/pallas_call | solution.py:281
  147.5 1.5 collective-permute-done.28
  149.0 7.0 %collective-permute-done.27 = bf16[128,4096]{1,0:T(8,128)(2,1)S(1)} collective-permute-done((bf16[128,4096]{1,0:T(8,128)(2,1)S(1)}, bf16[128,4096]{1,0:T(8,128)(2,1)S(1)}, u32[]{:S(2)}, u32[]{:S(2)}) %collective-permute-start.27) | collective-permute-done | bytes 1048608 | tf_op jit(solution)/shard_map/ppermute | solution.py:54
  156.0 1.3 add_convert_fusion
  (49 shorter events, 1.1 us)
Async XLA Ops:
  0.0 5.5 %copy-start.3 = (s32[4,8]{1,0:T(4,128)S(1)}, s32[4,8]{1,0:T(4,128)}, u32[]{:S(2)}) copy-start(s32[4,8]{1,0:T(4,128)} %param.12) | copy-start | bytes 388
  0.0 20.9 %copy-start = (bf16[4096,256]{1,0:T(8,128)(2,1)S(1)}, bf16[4096,256]{1,0:T(8,128)(2,1)}, u32[]{:S(2)}) copy-start(bf16[4096,256]{1,0:T(8,128)(2,1)} %wk.3) | copy-start | bytes 6291460
  2.2 13.8 %collective-permute-start.1 = (bf16[256,1024]{1,0:T(8,128)(2,1)}, bf16[256,1024]{1,0:T(8,128)(2,1)}, u32[]{:S(2)}, u32[]{:S(2)}) collective-permute-start(bf16[256,1024]{1,0:T(8,128)(2,1)} %get-tuple-element.38.refs_0_), channel_id=1, source_target_pairs={{0,1},{1,2},{2,3},{3,0},{4,7},{5,4},{6,5},{7,6},{8,9},{9,10},{10,1... | collective-permute-start | bytes 1572872 | tf_op jit(solution)/shard_map/ppermute | solution.py:54
  5.5 13.9 %collective-permute-start.2 = (bf16[256,1024]{1,0:T(8,128)(2,1)}, bf16[256,1024]{1,0:T(8,128)(2,1)}, u32[]{:S(2)}, u32[]{:S(2)}) collective-permute-start(bf16[256,1024]{1,0:T(8,128)(2,1)} %get-tuple-element.38.refs_0_), channel_id=1, source_target_pairs={{0,3},{1,0},{2,1},{3,2},{4,5},{5,6},{6,7},{7,4},{8,11},{9,8},{10,9... | collective-permute-start | bytes 1572872 | tf_op jit(solution)/shard_map/ppermute | solution.py:54
  5.5 2.8 %collective-permute-start = (s32[4,8]{1,0:T(4,128)S(1)}, s32[4,8]{1,0:T(4,128)S(1)}, u32[]{:S(2)}, u32[]{:S(2)}) collective-permute-start(s32[4,8]{1,0:T(4,128)S(1)} %copy-done.3), channel_id=1, source_target_pairs={{0,4},{4,0},{8,12},{12,8},{16,20},{20,16},{24,28},{28,24},{32,36},... | collective-permute-start | bytes 392 | tf_op jit(solution)/shard_map/ppermute | solution.py:50
  16.0 11.4 %collective-permute-start.3 = (bf16[256,1024]{1,0:T(8,128)(2,1)}, bf16[256,1024]{1,0:T(8,128)(2,1)S(1)}, u32[]{:S(2)}, u32[]{:S(2)}) collective-permute-start(bf16[256,1024]{1,0:T(8,128)(2,1)} %collective-permute-done.1.refs_1_), channel_id=1, source_target_pairs={{0,1},{1,2},{2,3},{3,0},{4,7},{5,4},{6,5},{7,6},{8,9},{9,10},{10,1... | collective-permute-start | bytes 1572872 | tf_op jit(solution)/shard_map/ppermute | solution.py:54
  19.4 21.7 %collective-permute-start.4 = (bf16[256,1024]{1,0:T(8,128)(2,1)S(1)}, bf16[256,1024]{1,0:T(8,128)(2,1)S(1)}, u32[]{:S(2)}, u32[]{:S(2)}) collective-permute-start(bf16[256,1024]{1,0:T(8,128)(2,1)S(1)} %get-tuple-element.28.refs_4_.refs_0_), channel_id=1, source_target_pairs={{0,1},{1,2},{2,3},{3,0},{4,7},{5,4},{6,5},{7,6},{8,9},{9,10},{10,1... | collective-permute-start | bytes 1572872 | tf_op jit(solution)/shard_map/ppermute | solution.py:54
  19.8 27.8 %collective-permute-start.5 = (bf16[256,1024]{1,0:T(8,128)(2,1)S(1)}, bf16[256,1024]{1,0:T(8,128)(2,1)S(1)}, u32[]{:S(2)}, u32[]{:S(2)}) collective-permute-start(bf16[256,1024]{1,0:T(8,128)(2,1)S(1)} %get-tuple-element.28.refs_4_.refs_0_), channel_id=1, source_target_pairs={{0,3},{1,0},{2,1},{3,2},{4,5},{5,6},{6,7},{7,4},{8,11},{9,8},{10,9... | collective-permute-start | bytes 1572872 | tf_op jit(solution)/shard_map/ppermute | solution.py:54
  20.9 1.6 %copy-start.1 = (bf16[4096,256]{1,0:T(8,128)(2,1)S(1)}, bf16[4096,256]{1,0:T(8,128)(2,1)}, u32[]{:S(2)}) copy-start(bf16[4096,256]{1,0:T(8,128)(2,1)} %wv.3) | copy-start | bytes 6291460
  28.5 7.8 %collective-permute-start.7 = (bf16[256,256]{1,0:T(8,128)(2,1)S(1)}, bf16[256,256]{1,0:T(8,128)(2,1)S(1)}, u32[]{:S(2)}, u32[]{:S(2)}) collective-permute-start(bf16[256,256]{1,0:T(8,128)(2,1)S(1)} %get-tuple-element.25), channel_id=1, source_target_pairs={{0,4},{4,0},{8,12},{12,8},{16,20},{20,16},{24,28},{28,24},{32,36},... | collective-permute-start | bytes 393224 | tf_op jit(solution)/shard_map/ppermute | solution.py:50
  36.3 7.2 %collective-permute-start.8 = (bf16[512,256]{1,0:T(8,128)(2,1)S(1)}, bf16[512,256]{1,0:T(8,128)(2,1)S(1)}, u32[]{:S(2)}, u32[]{:S(2)}) collective-permute-start(bf16[512,256]{1,0:T(8,128)(2,1)S(1)} %shard_map.76.refs_0_), channel_id=1, source_target_pairs={{0,32},{4,12},{8,40},{12,20},{16,48},{20,28},{24,56},{28,4},{32,64... | collective-permute-start | bytes 786440 | tf_op jit(solution)/shard_map/ppermute | solution.py:58
  38.1 7.6 %collective-permute-start.9 = (bf16[512,256]{1,0:T(8,128)(2,1)S(1)}, bf16[512,256]{1,0:T(8,128)(2,1)S(1)}, u32[]{:S(2)}, u32[]{:S(2)}) collective-permute-start(bf16[512,256]{1,0:T(8,128)(2,1)S(1)} %shard_map.76.refs_0_), channel_id=1, source_target_pairs={{0,96},{4,28},{8,104},{12,4},{16,112},{20,12},{24,120},{28,20},{32... | collective-permute-start | bytes 786440 | tf_op jit(solution)/shard_map/ppermute | solution.py:58
  39.6 8.0 %collective-permute-start.10 = (bf16[512,256]{1,0:T(8,128)(2,1)S(1)}, bf16[512,256]{1,0:T(8,128)(2,1)S(1)}, u32[]{:S(2)}, u32[]{:S(2)}) collective-permute-start(bf16[512,256]{1,0:T(8,128)(2,1)S(1)} %shard_map.76.refs_0_), channel_id=1, source_target_pairs={{0,64},{4,20},{8,72},{12,28},{16,80},{20,4},{24,88},{28,12},{32,96... | collective-permute-start | bytes 786440 | tf_op jit(solution)/shard_map/ppermute | solution.py:58
  41.1 8.5 %collective-permute-start.6 = (bf16[256,1024]{1,0:T(8,128)(2,1)S(1)}, bf16[256,1024]{1,0:T(8,128)(2,1)S(1)}, u32[]{:S(2)}, u32[]{:S(2)}) collective-permute-start(bf16[256,1024]{1,0:T(8,128)(2,1)S(1)} %collective-permute-done.4.refs_5_.refs_1_), channel_id=1, source_target_pairs={{0,1},{1,2},{2,3},{3,0},{4,7},{5,4},{6,5},{7,6},{8,9},{9,10},{10,1... | collective-permute-start | bytes 1572872 | tf_op jit(solution)/shard_map/ppermute | solution.py:54
  47.5 21.1 %slice-start = ((s8[8388608]{0:T(1024)(128)(4,1)}), s8[4194304]{0:T(1024)(128)(4,1)S(1)}, s32[]{:S(2)}) async-start(s8[8388608]{0:T(1024)(128)(4,1)} %bitcast.8), calls=%async_computation | async-start | bytes 8388608
  47.6 21.0 %slice-start.1 = ((s8[8388608]{0:T(1024)(128)(4,1)}), s8[4194304]{0:T(1024)(128)(4,1)S(1)}, s32[]{:S(2)}) async-start(s8[8388608]{0:T(1024)(128)(4,1)} %bitcast.8), calls=%async_computation.1 | async-start | bytes 8388608
  50.7 4.9 %collective-permute-start.14 = (bf16[256,256]{1,0:T(8,128)(2,1)S(1)}, bf16[256,256]{1,0:T(8,128)(2,1)S(1)}, u32[]{:S(2)}, u32[]{:S(2)}) collective-permute-start(bf16[256,256]{1,0:T(8,128)(2,1)S(1)} %get-tuple-element.32), channel_id=1, source_target_pairs={{0,4},{4,0},{8,12},{12,8},{16,20},{20,16},{24,28},{28,24},{32,36},... | collective-permute-start | bytes 393224 | tf_op jit(solution)/shard_map/ppermute | solution.py:50
  55.6 6.9 %collective-permute-start.15 = (bf16[512,256]{1,0:T(8,128)(2,1)S(1)}, bf16[512,256]{1,0:T(8,128)(2,1)S(1)}, u32[]{:S(2)}, u32[]{:S(2)}) collective-permute-start(bf16[512,256]{1,0:T(8,128)(2,1)S(1)} %shard_map.80.refs_0_), channel_id=1, source_target_pairs={{0,32},{4,12},{8,40},{12,20},{16,48},{20,28},{24,56},{28,4},{32,64... | collective-permute-start | bytes 786440 | tf_op jit(solution)/shard_map/ppermute | solution.py:58
  57.0 7.6 %collective-permute-start.16 = (bf16[512,256]{1,0:T(8,128)(2,1)S(1)}, bf16[512,256]{1,0:T(8,128)(2,1)S(1)}, u32[]{:S(2)}, u32[]{:S(2)}) collective-permute-start(bf16[512,256]{1,0:T(8,128)(2,1)S(1)} %shard_map.80.refs_0_), channel_id=1, source_target_pairs={{0,96},{4,28},{8,104},{12,4},{16,112},{20,12},{24,120},{28,20},{32... | collective-permute-start | bytes 786440 | tf_op jit(solution)/shard_map/ppermute | solution.py:58
  58.5 8.9 %collective-permute-start.17 = (bf16[512,256]{1,0:T(8,128)(2,1)S(1)}, bf16[512,256]{1,0:T(8,128)(2,1)S(1)}, u32[]{:S(2)}, u32[]{:S(2)}) collective-permute-start(bf16[512,256]{1,0:T(8,128)(2,1)S(1)} %shard_map.80.refs_0_), channel_id=1, source_target_pairs={{0,64},{4,20},{8,72},{12,28},{16,80},{20,4},{24,88},{28,12},{32,96... | collective-permute-start | bytes 786440 | tf_op jit(solution)/shard_map/ppermute | solution.py:58
  60.1 20.0 %collective-permute-start.11 = (bf16[2048,256]{1,0:T(8,128)(2,1)S(1)}, bf16[2048,256]{1,0:T(8,128)(2,1)S(1)}, u32[]{:S(2)}, u32[]{:S(2)}) collective-permute-start(bf16[2048,256]{1,0:T(8,128)(2,1)S(1)} %shard_map.77.rest_0_), channel_id=1, source_target_pairs={{0,8},{4,36},{8,16},{12,44},{16,24},{20,52},{24,0},{28,60},{32,40}... | collective-permute-start | bytes 3145736 | tf_op jit(solution)/shard_map/ppermute | solution.py:62
  67.5 14.0 %collective-permute-start.19 = (bf16[2048,256]{1,0:T(8,128)(2,1)S(1)}, bf16[2048,256]{1,0:T(8,128)(2,1)S(1)}, u32[]{:S(2)}, u32[]{:S(2)}) collective-permute-start(bf16[2048,256]{1,0:T(8,128)(2,1)S(1)} %shard_map.81.rest_4_), channel_id=1, source_target_pairs={{0,24},{4,100},{8,0},{12,108},{16,8},{20,116},{24,16},{28,124},{32... | collective-permute-start | bytes 3145736 | tf_op jit(solution)/shard_map/ppermute | solution.py:62
  68.3 24.4 %collective-permute-start.12 = (bf16[2048,256]{1,0:T(8,128)(2,1)S(1)}, bf16[2048,256]{1,0:T(8,128)(2,1)S(1)}, u32[]{:S(2)}, u32[]{:S(2)}) collective-permute-start(bf16[2048,256]{1,0:T(8,128)(2,1)S(1)} %shard_map.77.rest_0_), channel_id=1, source_target_pairs={{0,24},{4,100},{8,0},{12,108},{16,8},{20,116},{24,16},{28,124},{32... | collective-permute-start | bytes 3145736 | tf_op jit(solution)/shard_map/ppermute | solution.py:62
  73.7 31.6 %copy-start.2 = (s32[16]{0:T(128)S(1)}, s32[16]{0:T(128)}, u32[]{:S(2)}) copy-start(s32[16]{0:T(128)} %lengths.15) | copy-start | bytes 196
  78.8 15.2 %collective-permute-start.18 = (bf16[2048,256]{1,0:T(8,128)(2,1)S(1)}, bf16[2048,256]{1,0:T(8,128)(2,1)S(1)}, u32[]{:S(2)}, u32[]{:S(2)}) collective-permute-start(bf16[2048,256]{1,0:T(8,128)(2,1)S(1)} %shard_map.81.rest_4_), channel_id=1, source_target_pairs={{0,8},{4,36},{8,16},{12,44},{16,24},{20,52},{24,0},{28,60},{32,40}... | collective-permute-start | bytes 3145736 | tf_op jit(solution)/shard_map/ppermute | solution.py:62
  80.1 25.2 %collective-permute-start.13 = (bf16[2048,256]{1,0:T(8,128)(2,1)S(1)}, bf16[2048,256]{1,0:T(8,128)(2,1)S(1)}, u32[]{:S(2)}, u32[]{:S(2)}) collective-permute-start(bf16[2048,256]{1,0:T(8,128)(2,1)S(1)} %collective-permute-done.11.rest_1_), channel_id=1, source_target_pairs={{0,8},{4,36},{8,16},{12,44},{16,24},{20,52},{24,0},{28,60},{32,40}... | collective-permute-start | bytes 3145736 | tf_op jit(solution)/shard_map/ppermute | solution.py:62
  81.5 23.8 %collective-permute-start.20 = (bf16[2048,256]{1,0:T(8,128)(2,1)S(1)}, bf16[2048,256]{1,0:T(8,128)(2,1)S(1)}, u32[]{:S(2)}, u32[]{:S(2)}) collective-permute-start(bf16[2048,256]{1,0:T(8,128)(2,1)S(1)} %collective-permute-done.19.rest_6_), channel_id=1, source_target_pairs={{0,24},{4,100},{8,0},{12,108},{16,8},{20,116},{24,16},{28,124},{32... | collective-permute-start | bytes 3145736 | tf_op jit(solution)/shard_map/ppermute | solution.py:62
  83.2 7.6 %collective-permute-start.21 = (bf16[512,512]{1,0:T(8,128)(2,1)S(1)}, bf16[512,512]{1,0:T(8,128)(2,1)S(1)}, u32[]{:S(2)}, u32[]{:S(2)}) collective-permute-start(bf16[512,512]{1,0:T(8,128)(2,1)S(1)} %shard_map.82), channel_id=1, source_target_pairs={{0,4},{4,0},{8,12},{12,8},{16,20},{20,16},{24,28},{28,24},{32,36},... | collective-permute-start | bytes 1572872 | tf_op jit(solution)/shard_map/ppermute | solution.py:50
  105.3 10.9 %slice-start.2 = ((s8[8388608]{0:T(1024)(128)(4,1)}), s8[4194304]{0:T(1024)(128)(4,1)S(1)}, s32[]{:S(2)}) async-start(s8[8388608]{0:T(1024)(128)(4,1)} %bitcast.10), calls=%async_computation.2 | async-start | bytes 8388608
  107.6 8.6 %slice-start.3 = ((s8[8388608]{0:T(1024)(128)(4,1)}), s8[4194304]{0:T(1024)(128)(4,1)S(1)}, s32[]{:S(2)}) async-start(s8[8388608]{0:T(1024)(128)(4,1)} %bitcast.10), calls=%async_computation.3 | async-start | bytes 8388608
  107.6 8.6 %collective-permute-start.22 = (bf16[128,512]{1,0:T(8,128)(2,1)S(1)}, bf16[128,512]{1,0:T(8,128)(2,1)S(1)}, u32[]{:S(2)}, u32[]{:S(2)}) collective-permute-start(bf16[128,512]{1,0:T(8,128)(2,1)S(1)} %shard_map.84), channel_id=1, source_target_pairs={{0,4},{4,0},{8,12},{12,8},{16,20},{20,16},{24,28},{28,24},{32,36},... | collective-permute-start | bytes 393224 | tf_op jit(solution)/shard_map/ppermute | solution.py:50
  119.5 19.7 %collective-permute-start.26 = (bf16[128,4096]{1,0:T(8,128)(2,1)S(1)}, bf16[128,4096]{1,0:T(8,128)(2,1)S(1)}, u32[]{:S(2)}, u32[]{:S(2)}) collective-permute-start(bf16[128,4096]{1,0:T(8,128)(2,1)S(1)} %shard_map.85), channel_id=1, source_target_pairs={{0,1},{1,2},{2,3},{3,0},{4,7},{5,4},{6,5},{7,6},{8,9},{9,10},{10,1... | collective-permute-start | bytes 3145736 | tf_op jit(solution)/shard_map/ppermute | solution.py:54
  121.9 2.6 %collective-permute-start.23 = (bf16[128,512]{1,0:T(8,128)(2,1)S(1)}, bf16[128,512]{1,0:T(8,128)(2,1)S(1)}, u32[]{:S(2)}, u32[]{:S(2)}) collective-permute-start(bf16[128,512]{1,0:T(8,128)(2,1)S(1)} %shard_map.87), channel_id=1, source_target_pairs={{0,4},{4,0},{8,12},{12,8},{16,20},{20,16},{24,28},{28,24},{32,36},... | collective-permute-start | bytes 393224 | tf_op jit(solution)/shard_map/ppermute | solution.py:50
  127.8 21.2 %collective-permute-start.28 = (bf16[128,4096]{1,0:T(8,128)(2,1)S(1)}, bf16[128,4096]{1,0:T(8,128)(2,1)S(1)}, u32[]{:S(2)}, u32[]{:S(2)}) collective-permute-start(bf16[128,4096]{1,0:T(8,128)(2,1)S(1)} %shard_map.88), channel_id=1, source_target_pairs={{0,3},{1,0},{2,1},{3,2},{4,5},{5,6},{6,7},{7,4},{8,11},{9,8},{10,9... | collective-permute-start | bytes 3145736 | tf_op jit(solution)/shard_map/ppermute | solution.py:54
  131.6 4.3 %collective-permute-start.24 = (bf16[128,512]{1,0:T(8,128)(2,1)S(1)}, bf16[128,512]{1,0:T(8,128)(2,1)S(1)}, u32[]{:S(2)}, u32[]{:S(2)}) collective-permute-start(bf16[128,512]{1,0:T(8,128)(2,1)S(1)} %shard_map.90), channel_id=1, source_target_pairs={{0,4},{4,0},{8,12},{12,8},{16,20},{20,16},{24,28},{28,24},{32,36},... | collective-permute-start | bytes 393224 | tf_op jit(solution)/shard_map/ppermute | solution.py:50
  139.5 16.6 %collective-permute-start.27 = (bf16[128,4096]{1,0:T(8,128)(2,1)S(1)}, bf16[128,4096]{1,0:T(8,128)(2,1)S(1)}, u32[]{:S(2)}, u32[]{:S(2)}) collective-permute-start(bf16[128,4096]{1,0:T(8,128)(2,1)S(1)} %add_convert_fusion.1), channel_id=1, source_target_pairs={{0,1},{1,2},{2,3},{3,0},{4,7},{5,4},{6,5},{7,6},{8,9},{9,10},{10,1... | collective-permute-start | bytes 3145736 | tf_op jit(solution)/shard_map/ppermute | solution.py:54
  141.8 2.3 %collective-permute-start.25 = (bf16[128,512]{1,0:T(8,128)(2,1)S(1)}, bf16[128,512]{1,0:T(8,128)(2,1)S(1)}, u32[]{:S(2)}, u32[]{:S(2)}) collective-permute-start(bf16[128,512]{1,0:T(8,128)(2,1)S(1)} %shard_map.93), channel_id=1, source_target_pairs={{0,4},{4,0},{8,12},{12,8},{16,20},{20,16},{24,28},{28,24},{32,36},... | collective-permute-start | bytes 393224 | tf_op jit(solution)/shard_map/ppermute | solution.py:50
